TPU v7x, 128 devices: a whole 4x4x4 slice. The times are simulated.
128 devices in a mesh: span: 16 (over z, x_hi, core), vert: 8 (over y, x_lo).
Axes of the slice: x: 4 (x_hi: 2, x_lo: 2; x = x_hi * 2 + x_lo), y: 4, z: 4, core: 2. Of those that a mesh axis runs over, the one named last changes fastest.
Arguments:
- adjoint: float32 [19, 128, 128, 1024], P(None, 'span', 'vert'), may hold values from -6 to 6
- saved: bfloat16 [19, 128, 128, 1024], P(None, 'span', 'vert')
- solid: int32 [128, 128, 1024], P('span', 'vert'), may hold values 0 or 1
- send_cells: int32 [128, 128, 128], P(('span', 'vert')), may hold values from 0 to 131071
- send_dirs: int32 [128, 128, 128], P(('span', 'vert')), may hold values from 1 to 18
- send_weight: float32 [128, 128, 128], P(('span', 'vert')), may hold values from 0.5 to 2
- send_counts: int32 [128, 128], P(('span', 'vert')), may hold values from 0 to 128, as said below
- recv_slots: int32 [128, 128, 128], P(('span', 'vert')), may hold values from 0 to 4095
Outputs:
- adjoint_prev: float32 [19, 128, 128, 1024], P(None, 'span', 'vert')
- element_sens: float32 [524288], P(('span', 'vert'))
Inputs may be any that keep to these rules, and one draw needn't show every extreme that they name: `send_counts`: every device sends exactly 128 live links to one owner.
All inputs are finite; a program needn't handle non-finite values. No bound on the sum of `solid` on one device may be relied on, other than what follows from the above.
Results may differ from a plain program's by a relative error of at most 0.0003.
Values sent between devices are 32-bit elements; how exact they have to be, the bound alone decides.
No kernel may reach another device: no remote copies, remote signals or barrier semaphores. Data moves between devices by JAX's collectives and lax.ppermute only.
A program may use at most 192 MiB of HBM per device.

v0:
```python
import math

import jax
import jax.numpy as jnp
from jax import lax
from jax.sharding import PartitionSpec as P

ELEM_DEV = 4096


VECS = [
    (0, 0, 0),
    (1, 0, 0),
    (-1, 0, 0),
    (0, 1, 0),
    (0, -1, 0),
    (0, 0, 1),
    (0, 0, -1),
    (1, 1, 0),
    (-1, -1, 0),
    (1, -1, 0),
    (-1, 1, 0),
    (1, 0, 1),
    (-1, 0, -1),
    (1, 0, -1),
    (-1, 0, 1),
    (0, 1, 1),
    (0, -1, -1),
    (0, 1, -1),
    (0, -1, 1),
]
WEIGHTS = [1.0 / 3.0] + [1.0 / 18.0] * 6 + [1.0 / 36.0] * 12
OPPOSITE = [0, 2, 1, 4, 3, 6, 5, 8, 7, 10, 9, 12, 11, 14, 13, 16, 15, 18, 17]
OMEGA = 1.6


def extended_2(cells, sides, width, closed):
    for axis, dim in sides:
        count = lax.axis_size(axis)
        ends = count if closed else count - 1
        head = lax.slice_in_dim(cells, 0, width, axis=dim)
        tail = lax.slice_in_dim(cells, cells.shape[dim] - width, cells.shape[dim], axis=dim)
        cells = jnp.concatenate(
            [
                lax.ppermute(tail, axis, [(i, (i + 1) % count) for i in range(ends)]),
                cells,
                lax.ppermute(head, axis, [((i + 1) % count, i) for i in range(ends)]),
            ],
            axis=dim,
        )
    return cells


def stream(extended, rows_s, rows_v):
    pieces = []
    for i in range(19):
        cs, cv, cx = VECS[i]
        piece = extended[i, 1 + cs : 1 + cs + rows_s, 1 + cv : 1 + cv + rows_v, :]
        pieces.append(jnp.roll(piece, -cx, axis=-1))
    return jnp.stack(pieces, 0)


def collide(pulled, saved, solid):
    popul = saved.astype(jnp.float32)
    rho = popul[0]
    mom_s = jnp.zeros_like(rho)
    mom_v = jnp.zeros_like(rho)
    mom_x = jnp.zeros_like(rho)
    for i in range(1, 19):
        rho = rho + popul[i]
        cs, cv, cx = VECS[i]
        if cs != 0:
            mom_s = mom_s + cs * popul[i]
        if cv != 0:
            mom_v = mom_v + cv * popul[i]
        if cx != 0:
            mom_x = mom_x + cx * popul[i]
    vel_s = mom_s / rho
    vel_v = mom_v / rho
    vel_x = mom_x / rho
    usq = vel_s * vel_s + vel_v * vel_v + vel_x * vel_x
    g_rho = jnp.zeros_like(rho)
    g_s = jnp.zeros_like(rho)
    g_v = jnp.zeros_like(rho)
    g_x = jnp.zeros_like(rho)
    for i in range(19):
        cs, cv, cx = VECS[i]
        cu = cs * vel_s + cv * vel_v + cx * vel_x
        weighted = WEIGHTS[i] * pulled[i]
        g_rho = g_rho + weighted * (1.0 - 4.5 * cu * cu + 1.5 * usq)
        g_s = g_s + weighted * (3.0 * cs + 9.0 * cu * cs - 3.0 * vel_s)
        g_v = g_v + weighted * (3.0 * cv + 9.0 * cu * cv - 3.0 * vel_v)
        g_x = g_x + weighted * (3.0 * cx + 9.0 * cu * cx - 3.0 * vel_x)
    is_solid = solid == 1
    result = []
    for j in range(19):
        cs, cv, cx = VECS[j]
        fluid_term = (1.0 - OMEGA) * pulled[j] + OMEGA * (g_rho + cs * g_s + cv * g_v + cx * g_x)
        result.append(jnp.where(is_solid, pulled[OPPOSITE[j]], fluid_term))
    return jnp.stack(result, 0)


def differences(pulled):
    return jnp.stack([pulled[i] - pulled[OPPOSITE[i]] for i in range(19)], 0)


def element_sums(slots, received, elem_count):
    total = slots.shape[0]
    block = math.gcd(total, 1024)
    turns = total // block
    slot_blocks = slots.reshape(turns, block)
    value_blocks = received.reshape(turns, block)
    columns = jnp.arange(elem_count, dtype=jnp.int32)[None, :]

    def accumulate(sums, pair):
        slot_row, value_row = pair
        table = (slot_row[:, None] == columns).astype(jnp.float32)
        part = jnp.dot(
            value_row[None, :],
            table,
            precision=lax.Precision.HIGHEST,
            preferred_element_type=jnp.float32,
        )
        return (sums + part[0], None)

    sums, _ = lax.scan(
        accumulate, jnp.zeros((elem_count,), jnp.float32), (slot_blocks, value_blocks)
    )
    return sums


def body(adjoint, saved, solid, send_cells, send_dirs, send_weight, send_counts, recv_slots):
    rows_s = adjoint.shape[1]
    rows_v = adjoint.shape[2]
    wrapped = extended_2(adjoint, (("span", 1),), 1, True)
    extended = extended_2(wrapped, (("vert", 2),), 1, False)
    pulled = stream(extended, rows_s, rows_v)
    cell_count = rows_s * rows_v * adjoint.shape[3]
    flat_diff = differences(pulled).reshape(-1)
    cells = send_cells[0]
    dirs = send_dirs[0]
    picked = flat_diff[dirs * cell_count + cells]
    slot_count = cells.shape[-1]
    live = jnp.arange(slot_count, dtype=jnp.int32)[None, :] < send_counts[0][:, None]
    values = jnp.where(live, send_weight[0] * picked, jnp.float32(0.0))
    received = lax.all_to_all(values, ("span", "vert"), split_axis=0, concat_axis=0, tiled=True)
    sens = element_sums(recv_slots[0].reshape(-1), received.reshape(-1), ELEM_DEV)
    adjoint_prev = collide(pulled, saved, solid)
    return (adjoint_prev, sens)


def solution(mesh):
    return jax.shard_map(
        body,
        mesh=mesh,
        in_specs=(
            P(None, "span", "vert", None),
            P(None, "span", "vert", None),
            P("span", "vert", None),
            P(("span", "vert"), None, None),
            P(("span", "vert"), None, None),
            P(("span", "vert"), None, None),
            P(("span", "vert"), None),
            P(("span", "vert"), None, None),
        ),
        out_specs=(P(None, "span", "vert", None), P(("span", "vert"))),
        check_vma=False,
    )
```

profile of v0, /device:TPU:1, one launch (start us, length us, event | category | flops | bytes accessed | tf_op | source)
XLA Modules:
  0.0 527.0 jit_solution(9150782185969971813)
XLA Ops:
  0.6 3.0 fusion.128
  3.7 4.1 collective-permute-start.1
  7.8 2.3 slice_bitcast_fusion.24
  10.1 7.7 %convert_element_type.4 = f32[19,8,16,1024]{3,2,1,0:T(8,128)} convert(bf16[19,8,16,1024]{3,2,1,0:T(8,128)(2,1)} %param.11) | non-fusion elementwise | flops 2490368 | bytes 14942208 | tf_op jit(solution)/shard_map/convert_element_type | solution.py:64
  18.5 1.2 fusion.129
  19.7 6.1 %add_divide_fusion.2 = (f32[8,16,1024]{2,1,0:T(8,128)}, f32[8,16,1024]{2,1,0:T(8,128)}) fusion(f32[19,8,16,1024]{3,2,1,0:T(8,128)} %convert_element_type.4), kind=kLoop, calls=%fused_computation.270 | loop fusion | flops 4325376 | bytes 11010048 | tf_op jit(solution)/shard_map/div | solution.py:78
  27.1 4.8 collective-permute-done.1
  31.9 2.6 constant_dynamic-update-slice_fusion.3
  34.6 11.4 %constant_dynamic-update-slice_fusion.1 = (f32[19,9,16,1024]{3,2,1,0:T(8,128)}, f32[19,10,16,1024]{3,2,1,0:T(8,128)S(1)}, f32[19,9,16,1024]{3,2,1,0:T(8,128)}) fusion(f32[19,8,16,1024]{3,2,1,0:T(8,128)} %param.10, f32[19,10,16,1024]{3,2,1,0:T(8,128)S(1)} %get-tuple-element.103, f32[19,9,16,1024]{3,2,1,0:T(8,128)} %get-tuple-element.102), kind=kLoop, calls=%fused_computation.299 | loop fusion | bytes 39845888
  46.0 2.6 constant_dynamic-update-slice_fusion
  48.6 2.1 subtract_dynamic-update-slice_fusion.17
  50.7 2.9 subtract_dynamic-update-slice_fusion.16
  53.6 1.7 fusion.127
  55.3 1.3 collective-permute-start.2
  56.6 4.0 collective-permute-start.3
  61.4 11.2 %collective-permute-done.2 = f32[19,10,1,1024]{3,2,1,0:T(1,128)S(1)} collective-permute-done((f32[19,10,1,1024]{3,2,1,0:T(1,128)S(1)}, f32[19,10,1,1024]{3,2,1,0:T(1,128)S(1)}, u32[]{:S(2)}, u32[]{:S(2)}) %collective-permute-start.2) | collective-permute-done | bytes 778272 | tf_op jit(solution)/shard_map/ppermute | solution.py:47
  79.4 1.6 subtract_dynamic-update-slice_fusion.9
  84.1 11.8 %bitcast_dynamic-update-slice_fusion.18 = (f32[19,8,16,1024]{3,2,1,0:T(8,128)}, f32[8,16,1024]{2,1,0:T(8,128)S(1)}, f32[8,16,1024]{2,1,0:T(8,128)S(1)}, f32[8,16...) fusion(f32[19,8,16,1024]{3,2,1,0:T(8,128)} %param.10, ...), kind=kLoop, calls=%fused_computation.195 | loop fusion | flops 60293120 | bytes 23199744
  95.9 2.5 bitcast_dynamic-update-slice_fusion.17
  98.4 2.3 bitcast_dynamic-update-slice_fusion.16
  105.2 1.1 bitcast_dynamic-update-slice_fusion.11
  107.4 1.1 bitcast_dynamic-update-slice_fusion.9
  111.5 6.2 %copy.299 = f32[304,8,8,128]{3,1,2,0:T(8,128)} copy(f32[304,8,8,128]{3,2,1,0:T(8,128)S(1)} %bitcast.539) | data formatting | bytes 19922944
  117.7 260.8 %gather_fusion = f32[16384]{0:T(1024)} fusion(f32[2490368]{0:T(1024)} %bitcast.534, s32[16384]{0:T(1024)} %fusion.124), kind=kCustom, calls=%fused_computation | custom fusion | bytes 196608 | tf_op jit(solution)/shard_map/gather | solution.py:142
  378.5 1.7 compare_select_fusion
  380.2 31.8 %all-to-all-start = ((f32[128,1,128]{2,1,0:T(1,128)}), f32[128,1,128]{2,1,0:T(1,128)}, u32[]{:S(2)}, u32[]{:S(2)}) async-start(f32[128,1,128]{2,1,0:T(1,128)} %compare_select_fusion), calls=%async_computation | async-start | bytes 131072 | tf_op jit(solution)/shard_map/all_to_all | solution.py:146
  412.1 2.5 bitcast_dynamic-update-slice_fusion.7
  414.6 2.3 bitcast_dynamic-update-slice_fusion.6
  416.8 2.4 bitcast_dynamic-update-slice_fusion.5
  419.2 2.3 bitcast_dynamic-update-slice_fusion.4
  426.4 1.6 reduce.3
  428.1 98.3 %while.11 = (s32[]{:T(128)}, f32[4096]{0:T(1024)S(1)}, f32[16,1024]{1,0:T(8,128)S(1)}, s32[16,1024]{1,0:T(8,128)}, s32[]{:T(128)}, /*index=5*/s32[]{:T(128)}) while((s32[]{:T(128)}, f32[4096]{0:T(1024)S(1)}, f32[16,1024]{1,0:T(8,128)S(1)}, s32[16,1024]{1,0:T(8,128)}, s32[]{:T(128)}, /*index=5*/s32[]{:T(128)}) %tuple.92), condition=%wide.region_1.2_spmd.clone, body=%wide.region_0.1_spmd.clone.sunk | while | flops 54534144 | bytes 82007 | solution.py:126
  428.9 5.4 %fusion.136 = f32[1,4096]{1,0:T(1,128)S(1)} fusion(s32[1024]{0:T(1024)S(1)} %bitcast.542, f32[16,1024]{1,0:T(8,128)S(1)} %get-tuple-element.197, s32[]{:T(128)} %get-tuple-element.189), kind=kOutput, calls=%fused_computation.3.clone.1 | convolution fusion | flops 54525952 | bytes 24580 | tf_op jit(solution)/shard_map/while/body/eval_jaxpr/dot_general | solution.py:118
  435.0 5.4 %fusion.136 = f32[1,4096]{1,0:T(1,128)S(1)} fusion(s32[1024]{0:T(1024)S(1)} %bitcast.542, f32[16,1024]{1,0:T(8,128)S(1)} %get-tuple-element.197, s32[]{:T(128)} %get-tuple-element.189), kind=kOutput, calls=%fused_computation.3.clone.1 | convolution fusion | flops 54525952 | bytes 24580 | tf_op jit(solution)/shard_map/while/body/eval_jaxpr/dot_general | solution.py:118
  441.1 5.4 %fusion.136 = f32[1,4096]{1,0:T(1,128)S(1)} fusion(s32[1024]{0:T(1024)S(1)} %bitcast.542, f32[16,1024]{1,0:T(8,128)S(1)} %get-tuple-element.197, s32[]{:T(128)} %get-tuple-element.189), kind=kOutput, calls=%fused_computation.3.clone.1 | convolution fusion | flops 54525952 | bytes 24580 | tf_op jit(solution)/shard_map/while/body/eval_jaxpr/dot_general | solution.py:118
  447.3 5.4 %fusion.136 = f32[1,4096]{1,0:T(1,128)S(1)} fusion(s32[1024]{0:T(1024)S(1)} %bitcast.542, f32[16,1024]{1,0:T(8,128)S(1)} %get-tuple-element.197, s32[]{:T(128)} %get-tuple-element.189), kind=kOutput, calls=%fused_computation.3.clone.1 | convolution fusion | flops 54525952 | bytes 24580 | tf_op jit(solution)/shard_map/while/body/eval_jaxpr/dot_general | solution.py:118
  453.4 5.4 %fusion.136 = f32[1,4096]{1,0:T(1,128)S(1)} fusion(s32[1024]{0:T(1024)S(1)} %bitcast.542, f32[16,1024]{1,0:T(8,128)S(1)} %get-tuple-element.197, s32[]{:T(128)} %get-tuple-element.189), kind=kOutput, calls=%fused_computation.3.clone.1 | convolution fusion | flops 54525952 | bytes 24580 | tf_op jit(solution)/shard_map/while/body/eval_jaxpr/dot_general | solution.py:118
  459.6 5.4 %fusion.136 = f32[1,4096]{1,0:T(1,128)S(1)} fusion(s32[1024]{0:T(1024)S(1)} %bitcast.542, f32[16,1024]{1,0:T(8,128)S(1)} %get-tuple-element.197, s32[]{:T(128)} %get-tuple-element.189), kind=kOutput, calls=%fused_computation.3.clone.1 | convolution fusion | flops 54525952 | bytes 24580 | tf_op jit(solution)/shard_map/while/body/eval_jaxpr/dot_general | solution.py:118
  465.7 5.4 %fusion.136 = f32[1,4096]{1,0:T(1,128)S(1)} fusion(s32[1024]{0:T(1024)S(1)} %bitcast.542, f32[16,1024]{1,0:T(8,128)S(1)} %get-tuple-element.197, s32[]{:T(128)} %get-tuple-element.189), kind=kOutput, calls=%fused_computation.3.clone.1 | convolution fusion | flops 54525952 | bytes 24580 | tf_op jit(solution)/shard_map/while/body/eval_jaxpr/dot_general | solution.py:118
  471.9 5.4 %fusion.136 = f32[1,4096]{1,0:T(1,128)S(1)} fusion(s32[1024]{0:T(1024)S(1)} %bitcast.542, f32[16,1024]{1,0:T(8,128)S(1)} %get-tuple-element.197, s32[]{:T(128)} %get-tuple-element.189), kind=kOutput, calls=%fused_computation.3.clone.1 | convolution fusion | flops 54525952 | bytes 24580 | tf_op jit(solution)/shard_map/while/body/eval_jaxpr/dot_general | solution.py:118
  478.0 5.4 %fusion.136 = f32[1,4096]{1,0:T(1,128)S(1)} fusion(s32[1024]{0:T(1024)S(1)} %bitcast.542, f32[16,1024]{1,0:T(8,128)S(1)} %get-tuple-element.197, s32[]{:T(128)} %get-tuple-element.189), kind=kOutput, calls=%fused_computation.3.clone.1 | convolution fusion | flops 54525952 | bytes 24580 | tf_op jit(solution)/shard_map/while/body/eval_jaxpr/dot_general | solution.py:118
  484.1 5.4 %fusion.136 = f32[1,4096]{1,0:T(1,128)S(1)} fusion(s32[1024]{0:T(1024)S(1)} %bitcast.542, f32[16,1024]{1,0:T(8,128)S(1)} %get-tuple-element.197, s32[]{:T(128)} %get-tuple-element.189), kind=kOutput, calls=%fused_computation.3.clone.1 | convolution fusion | flops 54525952 | bytes 24580 | tf_op jit(solution)/shard_map/while/body/eval_jaxpr/dot_general | solution.py:118
  490.3 5.4 %fusion.136 = f32[1,4096]{1,0:T(1,128)S(1)} fusion(s32[1024]{0:T(1024)S(1)} %bitcast.542, f32[16,1024]{1,0:T(8,128)S(1)} %get-tuple-element.197, s32[]{:T(128)} %get-tuple-element.189), kind=kOutput, calls=%fused_computation.3.clone.1 | convolution fusion | flops 54525952 | bytes 24580 | tf_op jit(solution)/shard_map/while/body/eval_jaxpr/dot_general | solution.py:118
  496.4 5.4 %fusion.136 = f32[1,4096]{1,0:T(1,128)S(1)} fusion(s32[1024]{0:T(1024)S(1)} %bitcast.542, f32[16,1024]{1,0:T(8,128)S(1)} %get-tuple-element.197, s32[]{:T(128)} %get-tuple-element.189), kind=kOutput, calls=%fused_computation.3.clone.1 | convolution fusion | flops 54525952 | bytes 24580 | tf_op jit(solution)/shard_map/while/body/eval_jaxpr/dot_general | solution.py:118
  502.6 5.4 %fusion.136 = f32[1,4096]{1,0:T(1,128)S(1)} fusion(s32[1024]{0:T(1024)S(1)} %bitcast.542, f32[16,1024]{1,0:T(8,128)S(1)} %get-tuple-element.197, s32[]{:T(128)} %get-tuple-element.189), kind=kOutput, calls=%fused_computation.3.clone.1 | convolution fusion | flops 54525952 | bytes 24580 | tf_op jit(solution)/shard_map/while/body/eval_jaxpr/dot_general | solution.py:118
  508.7 5.4 %fusion.136 = f32[1,4096]{1,0:T(1,128)S(1)} fusion(s32[1024]{0:T(1024)S(1)} %bitcast.542, f32[16,1024]{1,0:T(8,128)S(1)} %get-tuple-element.197, s32[]{:T(128)} %get-tuple-element.189), kind=kOutput, calls=%fused_computation.3.clone.1 | convolution fusion | flops 54525952 | bytes 24580 | tf_op jit(solution)/shard_map/while/body/eval_jaxpr/dot_general | solution.py:118
  514.9 5.4 %fusion.136 = f32[1,4096]{1,0:T(1,128)S(1)} fusion(s32[1024]{0:T(1024)S(1)} %bitcast.542, f32[16,1024]{1,0:T(8,128)S(1)} %get-tuple-element.197, s32[]{:T(128)} %get-tuple-element.189), kind=kOutput, calls=%fused_computation.3.clone.1 | convolution fusion | flops 54525952 | bytes 24580 | tf_op jit(solution)/shard_map/while/body/eval_jaxpr/dot_general | solution.py:118
  521.0 5.4 %fusion.136 = f32[1,4096]{1,0:T(1,128)S(1)} fusion(s32[1024]{0:T(1024)S(1)} %bitcast.542, f32[16,1024]{1,0:T(8,128)S(1)} %get-tuple-element.197, s32[]{:T(128)} %get-tuple-element.189), kind=kOutput, calls=%fused_computation.3.clone.1 | convolution fusion | flops 54525952 | bytes 24580 | tf_op jit(solution)/shard_map/while/body/eval_jaxpr/dot_general | solution.py:118
  (146 shorter events, 38.8 us)
Async XLA Ops:
  3.7 14.2 %copy-start.26 = (s32[1,128,128]{2,1,0:T(8,128)S(1)}, s32[1,128,128]{2,1,0:T(8,128)}, u32[]{:S(2)}) copy-start(s32[1,128,128]{2,1,0:T(8,128)} %param.17) | copy-start | bytes 196612
  3.7 28.3 %collective-permute-start.1 = (f32[19,1,16,1024]{3,2,1,0:T(8,128)}, f32[19,1,16,1024]{3,2,1,0:T(8,128)}, u32[]{:S(2)}, u32[]{:S(2)}) collective-permute-start(f32[19,1,16,1024]{3,2,1,0:T(8,128)} %get-tuple-element.99), channel_id=1, source_target_pairs={{0,8},{8,16},{16,24},{24,32},{32,40},{40,48},{48,56},{56,64},{64,7... | collective-permute-start | bytes 3735560 | tf_op jit(solution)/shard_map/ppermute | solution.py:45
  7.8 38.2 %collective-permute-start = (f32[19,1,16,1024]{3,2,1,0:T(8,128)S(1)}, f32[19,1,16,1024]{3,2,1,0:T(8,128)}, u32[]{:S(2)}, u32[]{:S(2)}) collective-permute-start(f32[19,1,16,1024]{3,2,1,0:T(8,128)S(1)} %get-tuple-element.98), channel_id=1, source_target_pairs={{8,0},{16,8},{24,16},{32,24},{40,32},{48,40},{56,48},{64,56},{72,6... | collective-permute-start | bytes 3735560 | tf_op jit(solution)/shard_map/ppermute | solution.py:47
  17.8 7.9 %copy-start.24 = (s32[1,128,128]{2,1,0:T(8,128)S(1)}, s32[1,128,128]{2,1,0:T(8,128)}, u32[]{:S(2)}) copy-start(s32[1,128,128]{2,1,0:T(8,128)} %param.13) | copy-start | bytes 196612
  17.8 7.9 %copy-start.25 = (s32[1,128,128]{2,1,0:T(8,128)S(1)}, s32[1,128,128]{2,1,0:T(8,128)}, u32[]{:S(2)}) copy-start(s32[1,128,128]{2,1,0:T(8,128)} %param.14) | copy-start | bytes 196612
  55.3 17.3 %collective-permute-start.2 = (f32[19,10,1,1024]{3,2,1,0:T(1,128)S(1)}, f32[19,10,1,1024]{3,2,1,0:T(1,128)S(1)}, u32[]{:S(2)}, u32[]{:S(2)}) collective-permute-start(f32[19,10,1,1024]{3,2,1,0:T(1,128)S(1)} %get-tuple-element.85), channel_id=1, source_target_pairs={{1,0},{2,1},{3,2},{4,3},{5,4},{6,5},{7,6},{9,8},{10,9},{11,10},{12... | collective-permute-start | bytes 2334728 | tf_op jit(solution)/shard_map/ppermute | solution.py:47
  56.6 16.9 %collective-permute-start.3 = (f32[19,10,1,1024]{3,2,1,0:T(1,128)S(1)}, f32[19,10,1,1024]{3,2,1,0:T(1,128)S(1)}, u32[]{:S(2)}, u32[]{:S(2)}) collective-permute-start(f32[19,10,1,1024]{3,2,1,0:T(1,128)S(1)} %get-tuple-element.86), channel_id=1, source_target_pairs={{0,1},{1,2},{2,3},{3,4},{4,5},{5,6},{6,7},{8,9},{9,10},{10,11},{11... | collective-permute-start | bytes 2334728 | tf_op jit(solution)/shard_map/ppermute | solution.py:45
  61.1 20.7 %copy-start.6 = (f32[8,16,1023]{2,1,0:T(8,128)}, f32[8,16,1023]{2,1,0:T(8,128)S(1)}, u32[]{:S(2)}) copy-start(f32[8,16,1023]{2,1,0:T(8,128)S(1)} %get-tuple-element.137) | copy-start | bytes 1571332
  61.1 20.7 %copy-start.7 = (f32[8,16,1023]{2,1,0:T(8,128)}, f32[8,16,1023]{2,1,0:T(8,128)S(1)}, u32[]{:S(2)}) copy-start(f32[8,16,1023]{2,1,0:T(8,128)S(1)} %get-tuple-element.156) | copy-start | bytes 1571332
  61.4 20.5 %copy-start.4 = (f32[8,16,1023]{2,1,0:T(8,128)}, f32[8,16,1023]{2,1,0:T(8,128)S(1)}, u32[]{:S(2)}) copy-start(f32[8,16,1023]{2,1,0:T(8,128)S(1)} %get-tuple-element.127) | copy-start | bytes 1571332
  61.4 20.5 %copy-start.5 = (f32[8,16,1023]{2,1,0:T(8,128)}, f32[8,16,1023]{2,1,0:T(8,128)S(1)}, u32[]{:S(2)}) copy-start(f32[8,16,1023]{2,1,0:T(8,128)S(1)} %get-tuple-element.154) | copy-start | bytes 1571332
  78.4 3.4 slice-start
  79.4 3.1 slice-start.1
  79.4 3.9 slice-start.2
  79.4 4.1 copy-start.8
  79.4 4.2 copy-start.9
  79.4 4.3 copy-start.10
  79.4 4.5 copy-start.11
  79.4 4.5 copy-start.20
  79.4 4.5 copy-start.21
  79.4 4.6 copy-start.22
  81.2 14.7 %copy-start.12 = (f32[8,16,1]{2,1,0:T(8,128)}, f32[8,16,1]{2,1,0:T(8,128)S(1)}, u32[]{:S(2)}) copy-start(f32[8,16,1]{2,1,0:T(8,128)S(1)} %get-tuple-element.107) | copy-start | bytes 1540
  81.4 14.5 %copy-start.14 = (f32[8,16,1]{2,1,0:T(8,128)}, f32[8,16,1]{2,1,0:T(8,128)S(1)}, u32[]{:S(2)}) copy-start(f32[8,16,1]{2,1,0:T(8,128)S(1)} %get-tuple-element.113) | copy-start | bytes 1540
  81.6 14.3 %copy-start = (f32[8,16,1023]{2,1,0:T(8,128)}, f32[8,16,1023]{2,1,0:T(8,128)S(1)}, u32[]{:S(2)}) copy-start(f32[8,16,1023]{2,1,0:T(8,128)S(1)} %get-tuple-element.115) | copy-start | bytes 1571332
  81.6 14.2 %copy-start.16 = (f32[8,16,1]{2,1,0:T(8,128)}, f32[8,16,1]{2,1,0:T(8,128)S(1)}, u32[]{:S(2)}) copy-start(f32[8,16,1]{2,1,0:T(8,128)S(1)} %get-tuple-element.117) | copy-start | bytes 1540
  81.7 14.1 %copy-start.2 = (f32[8,16,1023]{2,1,0:T(8,128)}, f32[8,16,1023]{2,1,0:T(8,128)S(1)}, u32[]{:S(2)}) copy-start(f32[8,16,1023]{2,1,0:T(8,128)S(1)} %get-tuple-element.121) | copy-start | bytes 1571332
  81.8 14.1 %copy-start.18 = (f32[8,16,1]{2,1,0:T(8,128)}, f32[8,16,1]{2,1,0:T(8,128)S(1)}, u32[]{:S(2)}) copy-start(f32[8,16,1]{2,1,0:T(8,128)S(1)} %get-tuple-element.119) | copy-start | bytes 1540
  100.7 7.9 %slice-start.3 = ((s8[9961472]{0:T(1024)(128)(4,1)}), s8[4194304]{0:T(1024)(128)(4,1)S(1)}, s32[]{:S(2)}) async-start(s8[9961472]{0:T(1024)(128)(4,1)} %bitcast.537), calls=%async_computation.4 | async-start | bytes 8388608
  102.9 5.7 %slice-start.4 = ((s8[9961472]{0:T(1024)(128)(4,1)}), s8[4194304]{0:T(1024)(128)(4,1)S(1)}, s32[]{:S(2)}) async-start(s8[9961472]{0:T(1024)(128)(4,1)} %bitcast.537), calls=%async_computation.5 | async-start | bytes 8388608
  105.2 3.4 slice-start.5
  380.2 45.7 %all-to-all-start = ((f32[128,1,128]{2,1,0:T(1,128)}), f32[128,1,128]{2,1,0:T(1,128)}, u32[]{:S(2)}, u32[]{:S(2)}) async-start(f32[128,1,128]{2,1,0:T(1,128)} %compare_select_fusion), calls=%async_computation | async-start | bytes 131072 | tf_op jit(solution)/shard_map/all_to_all | solution.py:146
  412.0 9.5 %copy-start.1 = (f32[8,16,1023]{2,1,0:T(8,128)S(1)}, f32[8,16,1023]{2,1,0:T(8,128)}, u32[]{:S(2)}) copy-start(f32[8,16,1023]{2,1,0:T(8,128)} %copy-done) | copy-start | bytes 1571332
  412.0 9.5 %copy-start.3 = (f32[8,16,1023]{2,1,0:T(8,128)S(1)}, f32[8,16,1023]{2,1,0:T(8,128)}, u32[]{:S(2)}) copy-start(f32[8,16,1023]{2,1,0:T(8,128)} %copy-done.2) | copy-start | bytes 1571332
  412.0 9.5 %copy-start.17 = (f32[8,16,1]{2,1,0:T(8,128)S(1)}, f32[8,16,1]{2,1,0:T(8,128)}, u32[]{:S(2)}) copy-start(f32[8,16,1]{2,1,0:T(8,128)} %copy-done.16) | copy-start | bytes 1540
  412.0 9.5 %copy-start.19 = (f32[8,16,1]{2,1,0:T(8,128)S(1)}, f32[8,16,1]{2,1,0:T(8,128)}, u32[]{:S(2)}) copy-start(f32[8,16,1]{2,1,0:T(8,128)} %copy-done.18) | copy-start | bytes 1540
  412.0 11.7 %copy-start.13 = (f32[8,16,1]{2,1,0:T(8,128)S(1)}, f32[8,16,1]{2,1,0:T(8,128)}, u32[]{:S(2)}) copy-start(f32[8,16,1]{2,1,0:T(8,128)} %copy-done.12) | copy-start | bytes 1540
  412.1 11.7 %copy-start.15 = (f32[8,16,1]{2,1,0:T(8,128)S(1)}, f32[8,16,1]{2,1,0:T(8,128)}, u32[]{:S(2)}) copy-start(f32[8,16,1]{2,1,0:T(8,128)} %copy-done.14) | copy-start | bytes 1540
  526.4 0.6 copy-start.23
where the time goes:
time: 535 us; the launch traced here: 527 us
  local copies, waits for them, and re-layouts  308 us (58%)
  matrix products  85.8 us (16%)
  other arithmetic  73.7 us (14%)
  starting transfers between devices  41.2 us (8%)
  waiting for transfers between devices  17 us (3%)
    gather x1, local copies, waits for them, and re-layouts, body(): picked = flat_diff[dirs * cell_count + cells]  261 us
    dot_general x16, matrix products, accumulate(): jnp.dot(value_row[None, :], table, precision=lax.Precision.HIGHEST, prefe...  85.8 us
    unnamed x37, other arithmetic  52.2 us
    all_to_all x1, starting transfers between devices, body(): lax.all_to_all(values, ('span', 'vert'), split_axis=0, concat_axis=0, til...  31.8 us
    unnamed x69, local copies, waits for them, and re-layouts  23.1 us
    dynamic_slice x16, local copies, waits for them, and re-layouts, element_sums(): lax.scan(accumulate, jnp.zeros((elem_count,), jnp.float32), (slot_blocks,...  12.3 us
    ppermute x2, waiting for transfers between devices, extended_2(): lax.ppermute(head, axis, [((i + 1) % count, i) for i in range(ends)])  11.2 us
  transfers between devices with their start and end apart: 5, of which 3 were waited for; matrix products, arithmetic and copies ran while one was open for 9% of the time, Pallas kernels for 0%

commit v1 on v0

v1 whole, which is shorter than its diff:
```python
import jax
import jax.numpy as jnp
from jax import lax
from jax.experimental import pallas as pl
from jax.experimental.pallas import tpu as pltpu
from jax.sharding import PartitionSpec as P

Q = 19
CS = 8
CV = 16
NX = 1024
CAP = 128
OWNERS = 128
ELEM_DEV = 4096
PAIRS = 9
LANES = 128
COLS = NX // LANES
ROWS = PAIRS * CS * CV * COLS
OMEGA = 1.6

VECS = [
    (0, 0, 0),
    (1, 0, 0),
    (-1, 0, 0),
    (0, 1, 0),
    (0, -1, 0),
    (0, 0, 1),
    (0, 0, -1),
    (1, 1, 0),
    (-1, -1, 0),
    (1, -1, 0),
    (-1, 1, 0),
    (1, 0, 1),
    (-1, 0, -1),
    (1, 0, -1),
    (-1, 0, 1),
    (0, 1, 1),
    (0, -1, -1),
    (0, 1, -1),
    (0, -1, 1),
]
SPAN_UP = [i for i in range(Q) if VECS[i][0] == 1]
SPAN_DOWN = [i for i in range(Q) if VECS[i][0] == -1]
VERT_UP = [i for i in range(Q) if VECS[i][1] == 1]
VERT_DOWN = [i for i in range(Q) if VECS[i][1] == -1]

VMEM = pl.BlockSpec(memory_space=pltpu.VMEM)
SMEM = pl.BlockSpec(memory_space=pltpu.SMEM)
ANY = pl.BlockSpec(memory_space=pl.ANY)


def collide(pulled, sums, diffs, saved, is_solid, store):
    f = [saved(i) for i in range(Q)]
    e = [None] * PAIRS
    o = [None] * PAIRS
    for p in range(PAIRS):
        e[p] = f[2 * p + 1] + f[2 * p + 2]
        o[p] = f[2 * p + 1] - f[2 * p + 2]
    rho = f[0] + ((e[0] + e[1]) + (e[2] + e[3])) + ((e[4] + e[5]) + (e[6] + e[7]) + e[8])
    us = (o[0] + ((o[3] + o[4]) + (o[5] + o[6]))) / rho
    uv = (o[1] + ((o[3] - o[4]) + (o[7] + o[8]))) / rho
    ux = (o[2] + ((o[5] - o[6]) + (o[7] - o[8]))) / rho
    usq = us * us + uv * uv + ux * ux
    d0, d1, d2, d3, d4, d5, d6, d7, d8 = diffs
    s0, s1, s2, s3, s4, s5, s6, s7, s8 = sums
    w = 1.0 / 36.0
    s34 = s3 + s4
    s56 = s5 + s6
    s78 = s7 + s8
    two0 = 2.0 * s0
    two1 = 2.0 * s1
    two2 = 2.0 * s2
    m0 = 12.0 * pulled[0] + (two0 + two1 + two2) + (s34 + s56 + s78)
    mss = two0 + s34 + s56
    mvv = two1 + s34 + s78
    mxx = two2 + s56 + s78
    msv = s3 - s4
    msx = s5 - s6
    mvx = s7 - s8
    ms = 2.0 * d0 + ((d3 + d4) + (d5 + d6))
    mv = 2.0 * d1 + ((d3 - d4) + (d7 + d8))
    mx = 2.0 * d2 + ((d5 - d6) + (d7 - d8))
    as_ = mss * us + msv * uv + msx * ux
    av = msv * us + mvv * uv + mvx * ux
    ax = msx * us + mvx * uv + mxx * ux
    k = OMEGA * w
    g = (k * m0) * (1.0 + 1.5 * usq) - (4.5 * k) * (us * as_ + uv * av + ux * ax)
    gs = (3.0 * k) * ((ms + 3.0 * as_) - us * m0)
    gv = (3.0 * k) * ((mv + 3.0 * av) - uv * m0)
    gx = (3.0 * k) * ((mx + 3.0 * ax) - ux * m0)
    keep = 1.0 - OMEGA
    store(0, jnp.where(is_solid, pulled[0], keep * pulled[0] + g))
    along = [gs, gv, gx, gs + gv, gs - gv, gs + gx, gs - gx, gv + gx, gv - gx]
    for p in range(PAIRS):
        a = pulled[2 * p + 1]
        b = pulled[2 * p + 2]
        store(2 * p + 1, jnp.where(is_solid, b, keep * a + (g + along[p])))
        store(2 * p + 2, jnp.where(is_solid, a, keep * b + (g - along[p])))


def load_copies(adj, h_up, h_dn, wide, sem):
    copies = []
    for lo, hi in ((0, 1), (3, 7), (15, 19)):
        copies.append(pltpu.make_async_copy(adj.at[pl.ds(lo, hi - lo)], wide.at[pl.ds(lo, hi - lo)], sem.at[len(copies)]))
    for k, i in enumerate(SPAN_UP):
        copies.append(pltpu.make_async_copy(adj.at[i, pl.ds(1, CS - 1)], wide.at[i, pl.ds(0, CS - 1)], sem.at[len(copies)]))
        copies.append(pltpu.make_async_copy(h_up.at[k], wide.at[i, CS - 1], sem.at[len(copies)]))
    for k, i in enumerate(SPAN_DOWN):
        copies.append(pltpu.make_async_copy(adj.at[i, pl.ds(0, CS - 1)], wide.at[i, pl.ds(1, CS - 1)], sem.at[len(copies)]))
        copies.append(pltpu.make_async_copy(h_dn.at[k], wide.at[i, 0], sem.at[len(copies)]))
    return copies


N_LOAD = 23


def link_values(ridx, table, lidx, weight, out):
    sub = lax.broadcasted_iota(jnp.int32, (8, LANES), 0)
    lane = lax.broadcasted_iota(jnp.int32, (8, LANES), 1)
    rows_per_turn = 4

    def turn(tt, carry):
        for q in range(rows_per_turn):
            t = tt * rows_per_turn + q
            lrow = jnp.broadcast_to(lidx[pl.ds(t, 1), :], (8, LANES))
            acc = jnp.zeros((8, LANES), jnp.float32)
            for g in range(LANES // 8):
                v = jnp.broadcast_to(table[pl.ds(ridx[t, 8 * g], 1), :], (8, LANES))
                for j in range(1, 8):
                    row = table[pl.ds(ridx[t, 8 * g + j], 1), :]
                    v = jnp.where(sub == j, jnp.broadcast_to(row, (8, LANES)), v)
                res = jnp.take_along_axis(v, lrow, axis=1)
                acc = jnp.where(lane // 8 == g, res, acc)
            acc = jnp.where(lane % 8 == sub, acc, 0.0)
            out[pl.ds(t, 1), :] = jnp.sum(acc, axis=0, keepdims=True) * weight[pl.ds(t, 1), :]
        return carry

    lax.fori_loop(0, OWNERS // rows_per_turn, turn, 0)


def step_kernel(
    ridx, lidx, weight, h_up, h_dn, v_up, v_dn, c7, c8, c9, c10, adj, saved, solid,
    out, values, wide, sav, sol, table, obuf, vup, vdn, load_sem, misc_sem, out_sem,
):
    copies = load_copies(adj, h_up, h_dn, wide, load_sem)
    for c in copies:
        c.start()
    misc = [
        pltpu.make_async_copy(saved, sav, misc_sem.at[0]),
        pltpu.make_async_copy(solid, sol, misc_sem.at[1]),
    ]
    for c in misc:
        c.start()
    for halo, rims, pops, corner in (
        (v_up, vup, VERT_UP, {7: c7, 10: c10}),
        (v_dn, vdn, VERT_DOWN, {8: c8, 9: c9}),
    ):
        for k, i in enumerate(pops):
            cs = VECS[i][0]
            for xt in range(COLS):
                span = slice(LANES * xt, LANES * (xt + 1))
                if cs == 0:
                    rims[k, xt] = halo[k, :, span]
                elif cs == 1:
                    rims[k, xt, 0 : CS - 1] = halo[k, 1:CS, span]
                    rims[k, xt, CS - 1 : CS] = corner[i][:, span]
                else:
                    rims[k, xt, 1:CS] = halo[k, 0 : CS - 1, span]
                    rims[k, xt, 0:1] = corner[i][:, span]
    for c in copies:
        c.wait()
    for c in misc:
        c.wait()

    vrow = lax.broadcasted_iota(jnp.int32, (CV, LANES), 0)
    lane = lax.broadcasted_iota(jnp.int32, (CV, LANES), 1)

    def slab(s, carry):
        rolled = {}

        def column(i, xt):
            cv = VECS[i][1]
            x = wide[i, s, :, LANES * xt : LANES * (xt + 1)]
            if cv == 1:
                rim = vup[VERT_UP.index(i), xt, pl.ds(s, 1), :]
                x = jnp.where(vrow == CV - 1, jnp.broadcast_to(rim, (CV, LANES)), pltpu.roll(x, CV - 1, 0))
            elif cv == -1:
                rim = vdn[VERT_DOWN.index(i), xt, pl.ds(s, 1), :]
                x = jnp.where(vrow == 0, jnp.broadcast_to(rim, (CV, LANES)), pltpu.roll(x, 1, 0))
            return x

        def rolled_column(i, xt):
            if (i, xt) not in rolled:
                rolled[i, xt] = pltpu.roll(column(i, xt), LANES - 1 if VECS[i][2] == 1 else 1, 1)
            return rolled[i, xt]

        for xt in range(COLS):
            pulled = []
            for i in range(Q):
                cx = VECS[i][2]
                if cx == 0:
                    pulled.append(column(i, xt))
                else:
                    here = rolled_column(i, xt)
                    beside = rolled_column(i, (xt + cx) % COLS)
                    edge = LANES - 1 if cx == 1 else 0
                    pulled.append(jnp.where(lane == edge, beside, here))
            sums = [pulled[2 * p + 1] + pulled[2 * p + 2] for p in range(PAIRS)]
            diffs = [pulled[2 * p + 1] - pulled[2 * p + 2] for p in range(PAIRS)]
            for p in range(PAIRS):
                for vt in range(2):
                    base = ((p * CS) * 2 + vt) * 64 + 8 * xt
                    table[pl.ds(pl.multiple_of(s * 128 + base, 8), 8), :] = diffs[p][8 * vt : 8 * vt + 8]

            def store(i, v):
                obuf[i, s, :, LANES * xt : LANES * (xt + 1)] = v

            collide(
                pulled, sums, diffs,
                lambda i: sav[i, s, :, LANES * xt : LANES * (xt + 1)].astype(jnp.float32),
                sol[s, :, LANES * xt : LANES * (xt + 1)] == 1,
                store,
            )
        pltpu.make_async_copy(obuf.at[:, s], out.at[:, s], out_sem.at[s]).start()
        return carry

    lax.fori_loop(0, CS, slab, 0)
    link_values(ridx, table, lidx, weight, values)
    for s in range(CS):
        pltpu.make_async_copy(obuf.at[:, s], out.at[:, s], out_sem.at[s]).wait()


def sums_kernel(slots, received, out):
    his = ELEM_DEV // LANES
    sub_lo = lax.broadcasted_iota(jnp.int32, (LANES, 2 * LANES), 0)
    sub_hi = lax.broadcasted_iota(jnp.int32, (his, 2 * LANES), 0)
    rows = OWNERS * CAP // (2 * LANES)

    def turn(t, acc):
        for q in range(4):
            r = t * 4 + q
            slot = slots[pl.ds(r, 1), :]
            v0 = received[pl.ds(r, 1), :]
            a = v0.astype(jnp.bfloat16).astype(jnp.float32)
            b = (v0 - a).astype(jnp.bfloat16).astype(jnp.float32)
            c = (v0 - a) - b
            hit = jnp.broadcast_to(slot >> 7, (his, 2 * LANES)) == sub_hi
            left = jnp.concatenate(
                [jnp.where(hit, jnp.broadcast_to(v, (his, 2 * LANES)), 0.0).astype(jnp.bfloat16) for v in (a, b, c)], 0
            )
            right = jnp.where(jnp.broadcast_to(slot & 127, (LANES, 2 * LANES)) == sub_lo, 1.0, 0.0).astype(jnp.bfloat16)
            acc = acc + lax.dot_general(
                left, right, (((1,), (1,)), ((), ())), preferred_element_type=jnp.float32
            )
        return acc

    acc = lax.fori_loop(0, rows // 4, turn, jnp.zeros((3 * his, LANES), jnp.float32))
    out[...] = acc[0:his] + acc[his : 2 * his] + acc[2 * his : 3 * his]


def halos(adjoint):
    ns = lax.axis_size("span")
    nv = lax.axis_size("vert")
    down = [(i, (i - 1) % ns) for i in range(ns)]
    up = [(i, (i + 1) % ns) for i in range(ns)]
    h_up = lax.ppermute(jnp.stack([adjoint[i, 0] for i in SPAN_UP], 0), "span", down)
    h_dn = lax.ppermute(jnp.stack([adjoint[i, CS - 1] for i in SPAN_DOWN], 0), "span", up)
    v_up = lax.ppermute(
        jnp.stack([adjoint[i, :, 0] for i in VERT_UP], 0), "vert", [(i, i - 1) for i in range(1, nv)]
    )
    v_dn = lax.ppermute(
        jnp.stack([adjoint[i, :, CV - 1] for i in VERT_DOWN], 0), "vert", [(i, i + 1) for i in range(nv - 1)]
    )
    corners = []
    for i in (7, 8, 9, 10):
        cs, cv, _ = VECS[i]
        pairs = []
        for a in range(ns):
            for b in range(nv):
                if 0 <= b + cv < nv:
                    pairs.append((((a + cs) % ns) * nv + b + cv, a * nv + b))
        piece = adjoint[i, 0 if cs == 1 else CS - 1, 0 if cv == 1 else CV - 1][None, :]
        corners.append(lax.ppermute(piece, ("span", "vert"), pairs))
    return h_up, h_dn, v_up, v_dn, corners


def body(adjoint, saved, solid, send_cells, send_dirs, send_weight, send_counts, recv_slots):
    h_up, h_dn, v_up, v_dn, corners = halos(adjoint)
    cells = send_cells[0]
    dirs = send_dirs[0]
    x_col = (cells >> 7) & 7
    v = (cells >> 10) & 15
    s = cells >> 14
    ridx = ((dirs - 1) >> 1) * 1024 + s * 128 + (v >> 3) * 64 + x_col * 8 + (v & 7)
    lidx = cells & 127
    live = jnp.arange(CAP, dtype=jnp.int32)[None, :] < send_counts[0][:, None]
    signed = jnp.where(dirs & 1 == 1, send_weight[0], -send_weight[0])
    weight = jnp.where(live, signed, 0.0)
    adjoint_prev, values = pl.pallas_call(
        step_kernel,
        out_shape=(
            jax.ShapeDtypeStruct((Q, CS, CV, NX), jnp.float32),
            jax.ShapeDtypeStruct((OWNERS, CAP), jnp.float32),
        ),
        in_specs=[SMEM, VMEM, VMEM, ANY, ANY, VMEM, VMEM, VMEM, VMEM, VMEM, VMEM, ANY, ANY, ANY],
        out_specs=(ANY, VMEM),
        scratch_shapes=[
            pltpu.VMEM((Q, CS, CV, NX), jnp.float32),
            pltpu.VMEM((Q, CS, CV, NX), jnp.bfloat16),
            pltpu.VMEM((CS, CV, NX), jnp.int32),
            pltpu.VMEM((ROWS, LANES), jnp.float32),
            pltpu.VMEM((Q, CS, CV, NX), jnp.float32),
            pltpu.VMEM((5, COLS, CS, LANES), jnp.float32),
            pltpu.VMEM((5, COLS, CS, LANES), jnp.float32),
            pltpu.SemaphoreType.DMA((N_LOAD,)),
            pltpu.SemaphoreType.DMA((2,)),
            pltpu.SemaphoreType.DMA((CS,)),
        ],
        compiler_params=pltpu.CompilerParams(vmem_limit_bytes=44 << 20),
        name="step",
    )(ridx, lidx, weight, h_up, h_dn, v_up, v_dn, *corners, adjoint, saved, solid)
    received = lax.all_to_all(values, ("span", "vert"), split_axis=0, concat_axis=0, tiled=True)
    sens = pl.pallas_call(
        sums_kernel,
        out_shape=jax.ShapeDtypeStruct((ELEM_DEV // LANES, LANES), jnp.float32),
        in_specs=[VMEM, VMEM],
        out_specs=VMEM,
        name="element_sums",
    )(recv_slots[0].reshape(64, 256), received.reshape(64, 256))
    return adjoint_prev, sens.reshape(ELEM_DEV)


def solution(mesh):
    return jax.shard_map(
        body,
        mesh=mesh,
        in_specs=(
            P(None, "span", "vert", None),
            P(None, "span", "vert", None),
            P("span", "vert", None),
            P(("span", "vert"), None, None),
            P(("span", "vert"), None, None),
            P(("span", "vert"), None, None),
            P(("span", "vert"), None),
            P(("span", "vert"), None, None),
        ),
        out_specs=(P(None, "span", "vert", None), P(("span", "vert"))),
        check_vma=False,
    )
```

time: 535 us -> 100 us (0.19); the launches traced: 527 us -> 99.2 us
  local copies, waits for them, and re-layouts: 308 us -> 12.6 us
  matrix products: 85.8 us -> 0 us
  other arithmetic: 73.7 us -> 2.67 us
  Pallas kernels: 0 us -> 32.5 us
  starting transfers between devices: 41.2 us -> 34.2 us
    gather x1 -> x0, local copies, waits for them, and re-layouts: 261 us -> none  [body(): picked = flat_diff[dirs * cell_count + cells]]
    dot_general x16 -> x0, matrix products: 85.8 us -> none  [accumulate(): jnp.dot(value_row[None, :], table, precision=lax.Precision.HIGHEST, prefe...]
    unnamed x37 -> x0, other arithmetic: 52.2 us -> none
    pallas_call x0 -> x2, Pallas kernels: none -> 32.5 us  [the longest x1 27.3 us: body(): pl.pallas_call(step_kernel, out_shape=(jax.ShapeDtypeStruct((Q, CS, CV, N...]
    all_to_all x1, starting transfers between devices: 31.8 us -> 8.49 us  [body(): lax.all_to_all(values, ('span', 'vert'), split_axis=0, concat_axis=0, til...]
    ppermute x4 -> x8, starting transfers between devices: 9.46 us -> 25.7 us  [the longest x4 15.2 us: halos(): corners.append(lax.ppermute(piece, ('span', 'vert'), pairs))]
    unnamed x69 -> x18, local copies, waits for them, and re-layouts: 23.1 us -> 7.09 us
    dynamic_slice x16 -> x0, local copies, waits for them, and re-layouts: 12.3 us -> none  [element_sums(): lax.scan(accumulate, jnp.zeros((elem_count,), jnp.float32), (slot_blocks,...]
  transfers between devices with their start and end apart: 5 -> 9, of which waited for: 3 -> 2; matrix products, arithmetic and copies ran while one was open for 9% -> 5% of each run, Pallas kernels for 0% -> 0%
where the time goes in v1:
time: 100 us; the launch traced here: 99.2 us
  starting transfers between devices  34.2 us (34%)
  Pallas kernels  32.5 us (32%)
  waiting for transfers between devices  16.3 us (16%)
  local copies, waits for them, and re-layouts  12.6 us (13%)
  other arithmetic  2.67 us (3%)
    pallas_call x1, Pallas kernels, body(): pl.pallas_call(step_kernel, out_shape=(jax.ShapeDtypeStruct((Q, CS, CV, N...  27.3 us
    ppermute x4, starting transfers between devices, halos(): corners.append(lax.ppermute(piece, ('span', 'vert'), pairs))  15.2 us
    all_to_all x1, waiting for transfers between devices, body(): lax.all_to_all(values, ('span', 'vert'), split_axis=0, concat_axis=0, til...  9.04 us
    all_to_all x1, starting transfers between devices, body(): lax.all_to_all(values, ('span', 'vert'), split_axis=0, concat_axis=0, til...  8.49 us
    ppermute x4, waiting for transfers between devices, halos(): corners.append(lax.ppermute(piece, ('span', 'vert'), pairs))  7.28 us
    unnamed x18, local copies, waits for them, and re-layouts  7.09 us
    pallas_call x1, Pallas kernels, body(): pl.pallas_call(sums_kernel, out_shape=jax.ShapeDtypeStruct((ELEM_DEV // L...  5.12 us
    ppermute x1, starting transfers between devices, halos(): lax.ppermute(jnp.stack([adjoint[i, :, CV - 1] for i in VERT_DOWN], 0), 'v...  4.97 us
  transfers between devices with their start and end apart: 9, of which 2 were waited for; matrix products, arithmetic and copies ran while one was open for 5% of the time, Pallas kernels for 0%

profile of v1, /device:TPU:1, one launch (start us, length us, event | category | flops | bytes accessed | tf_op | source)
XLA Modules:
  0.0 99.2 jit_solution(14365137709494031703)
XLA Ops:
  0.6 0.0 copy-start.2
  0.6 0.9 bitcast_dynamic-update-slice_fusion.4
  1.6 0.9 bitcast_dynamic-update-slice_fusion.3
  2.4 0.9 bitcast_dynamic-update-slice_fusion.2
  3.3 0.9 bitcast_dynamic-update-slice_fusion.1
  4.2 0.9 bitcast_dynamic-update-slice_fusion
  5.1 1.5 %collective-permute-start = (f32[5,16,1024]{2,1,0:T(8,128)S(1)}, f32[5,16,1024]{2,1,0:T(8,128)S(1)}, u32[]{:S(2)}, u32[]{:S(2)}) collective-permute-start(f32[5,16,1024]{2,1,0:T(8,128)S(1)} %get-tuple-element.21), channel_id=1, source_target_pairs={{0,120},{8,0},{16,8},{24,16},{32,24},{40,32},{48,40},{56,48},{64,5... | collective-permute-start | bytes 983048 | tf_op jit(solution)/shard_map/ppermute | solution.py:266
  6.6 2.8 %collective-permute-start.1 = (f32[5,16,1024]{2,1,0:T(8,128)S(1)}, f32[5,16,1024]{2,1,0:T(8,128)S(1)}, u32[]{:S(2)}, u32[]{:S(2)}) collective-permute-start(f32[5,16,1024]{2,1,0:T(8,128)S(1)} %get-tuple-element.20), channel_id=1, source_target_pairs={{0,8},{8,16},{16,24},{24,32},{32,40},{40,48},{48,56},{56,64},{64,7... | collective-permute-start | bytes 983048 | tf_op jit(solution)/shard_map/ppermute | solution.py:267
  9.4 0.8 slice_bitcast_fusion
  10.2 1.3 %collective-permute-start.4 = (f32[1,1024]{1,0:T(1,128)S(1)}, f32[1,1024]{1,0:T(1,128)S(1)}, u32[]{:S(2)}, u32[]{:S(2)}) collective-permute-start(f32[1,1024]{1,0:T(1,128)S(1)} %get-tuple-element.7), channel_id=1, source_target_pairs={{9,0},{10,1},{11,2},{12,3},{13,4},{14,5},{15,6},{17,8},{18,9},{19,... | collective-permute-start | bytes 12296 | tf_op jit(solution)/shard_map/ppermute | solution.py:283
  11.5 5.5 %collective-permute-start.5 = (f32[1,1024]{1,0:T(1,128)S(1)}, f32[1,1024]{1,0:T(1,128)S(1)}, u32[]{:S(2)}, u32[]{:S(2)}) collective-permute-start(f32[1,1024]{1,0:T(1,128)S(1)} %get-tuple-element.8), channel_id=1, source_target_pairs={{120,1},{121,2},{122,3},{123,4},{124,5},{125,6},{126,7},{0,9},{1,1... | collective-permute-start | bytes 12296 | tf_op jit(solution)/shard_map/ppermute | solution.py:283
  17.0 7.1 %collective-permute-start.6 = (f32[1,1024]{1,0:T(1,128)S(1)}, f32[1,1024]{1,0:T(1,128)S(1)}, u32[]{:S(2)}, u32[]{:S(2)}) collective-permute-start(f32[1,1024]{1,0:T(1,128)S(1)} %get-tuple-element.9), channel_id=1, source_target_pairs={{8,1},{9,2},{10,3},{11,4},{12,5},{13,6},{14,7},{16,9},{17,10},{18,... | collective-permute-start | bytes 12296 | tf_op jit(solution)/shard_map/ppermute | solution.py:283
  24.1 2.0 %fusion.2 = (f32[1,8,1,1024]{3,2,1,0:T(1,128)S(1)}, f32[1,8,1,1024]{3,2,1,0:T(1,128)S(1)}, f32[1,8,1,1024]{3,2,1,0:T(1,128)S(1)}, f32[1,8,1,1024]{3,2,1,0:T(1,12...) fusion(f32[19,8,16,1024]{3,2,1,0:T(8,128)} %adj.1), kind=kLoop, calls=%fused_computation.41 | loop fusion | bytes 655360 | tf_op jit(solution)/shard_map/slice | solution.py:272
  26.3 0.9 and_bitcast_fusion
  27.2 0.0 collective-permute-done.4.c7
  27.2 1.3 %collective-permute-start.2 = (f32[5,8,1024]{2,1,0:T(8,128)S(1)}, f32[5,8,1024]{2,1,0:T(8,128)S(1)}, u32[]{:S(2)}, u32[]{:S(2)}) collective-permute-start(f32[5,8,1024]{2,1,0:T(8,128)S(1)} %constant_dynamic-update-slice_fusion), channel_id=1, source_target_pairs={{1,0},{2,1},{3,2},{4,3},{5,4},{6,5},{7,6},{9,8},{10,9},{11,10},{12... | collective-permute-start | bytes 491528 | tf_op jit(solution)/shard_map/ppermute | solution.py:268
  28.5 0.0 collective-permute-done.5.c8
  28.5 5.0 %collective-permute-start.3 = (f32[5,8,1024]{2,1,0:T(8,128)S(1)}, f32[5,8,1024]{2,1,0:T(8,128)S(1)}, u32[]{:S(2)}, u32[]{:S(2)}) collective-permute-start(f32[5,8,1024]{2,1,0:T(8,128)S(1)} %constant_dynamic-update-slice_fusion.5), channel_id=1, source_target_pairs={{0,1},{1,2},{2,3},{3,4},{4,5},{5,6},{6,7},{8,9},{9,10},{10,11},{11... | collective-permute-start | bytes 491528 | tf_op jit(solution)/shard_map/ppermute | solution.py:271
  33.5 0.0 collective-permute-done.6.c9
  33.5 1.3 %collective-permute-start.7 = (f32[1,1024]{1,0:T(1,128)S(1)}, f32[1,1024]{1,0:T(1,128)S(1)}, u32[]{:S(2)}, u32[]{:S(2)}) collective-permute-start(f32[1,1024]{1,0:T(1,128)S(1)} %get-tuple-element.6), channel_id=1, source_target_pairs={{121,0},{122,1},{123,2},{124,3},{125,4},{126,5},{127,6},{1,8},{2,9... | collective-permute-start | bytes 12296 | tf_op jit(solution)/shard_map/ppermute | solution.py:283
  34.8 1.0 fusion.weight
  35.8 7.3 %collective-permute-done.7.c10 = f32[1,1024]{1,0:T(1,128)S(1)} collective-permute-done((f32[1,1024]{1,0:T(1,128)S(1)}, f32[1,1024]{1,0:T(1,128)S(1)}, u32[]{:S(2)}, u32[]{:S(2)}) %collective-permute-start.7) | collective-permute-done | bytes 4128 | tf_op jit(solution)/shard_map/ppermute | solution.py:283
  43.0 0.0 collective-permute-done.2.v_up
  43.0 0.0 collective-permute-done.3.v_dn
  43.0 0.0 collective-permute-done.h_up
  43.1 0.0 collective-permute-done.1.h_dn
  43.1 0.0 copy-start
  43.1 2.4 %copy-done = bf16[19,8,16,1024]{3,2,1,0:T(8,128)(2,1)S(1)} copy-done((bf16[19,8,16,1024]{3,2,1,0:T(8,128)(2,1)S(1)}, bf16[19,8,16,1024]{3,2,1,0:T(8,128)(2,1)}, u32[]{:S(2)}) %copy-start) | copy-done | bytes 4980760
  45.5 0.0 copy-start.1
  45.5 1.0 %copy-done.1 = s32[8,16,1024]{2,1,0:T(8,128)S(1)} copy-done((s32[8,16,1024]{2,1,0:T(8,128)S(1)}, s32[8,16,1024]{2,1,0:T(8,128)}, u32[]{:S(2)}) %copy-start.1) | copy-done | bytes 524312
  46.5 27.3 %step.1 = (f32[19,8,16,1024]{3,2,1,0:T(8,128)}, f32[128,128]{1,0:T(8,128)}) custom-call(s32[128,128]{1,0:T(8,128)S(1)} %get-tuple-element.31.ridx, s32[128,128]{1,0:T(8,128)S(1)} %get-tuple-element.30.lidx, f32[128,128]{1,0:T(8,128)S(1)} %fusion.weight, f32[5,16,1024]{2,1,0:T(8,128)S(1)} %collective-permute-done.h_up, ...), custom_call_target="tpu_custom_call" | custom-call | tf_op jit(solution)/shard_map/step/pallas_call | solution.py:299
  73.9 8.5 %all-to-all-start = ((f32[128,1,128]{2,1,0:T(1,128)}), f32[128,1,128]{2,1,0:T(1,128)S(1)}, u32[]{:S(2)}, u32[]{:S(2)}) async-start(f32[128,1,128]{2,1,0:T(1,128)} %bitcast.30), calls=%async_computation | async-start | bytes 131072 | tf_op jit(solution)/shard_map/all_to_all | solution.py:322
  82.4 0.0 copy-done.2
  82.4 0.6 reshape_squeeze.3.slots
  83.0 9.0 %all-to-all-done = f32[128,1,128]{2,1,0:T(1,128)S(1)} async-done(((f32[128,1,128]{2,1,0:T(1,128)}), f32[128,1,128]{2,1,0:T(1,128)S(1)}, u32[]{:S(2)}, u32[]{:S(2)}) %all-to-all-start) | async-done | bytes 65568 | tf_op jit(solution)/shard_map/all_to_all | solution.py:322
  92.1 0.5 broadcast.50
  92.6 0.8 reduce.3
  93.4 0.6 reshape.47.received
  94.0 5.1 %element_sums.1 = f32[32,128]{1,0:T(8,128)} custom-call(s32[64,256]{1,0:T(8,128)} %reshape_squeeze.3.slots, f32[64,256]{1,0:T(8,128)} %reshape.47.received), custom_call_target="tpu_custom_call" | custom-call | tf_op jit(solution)/shard_map/element_sums/pallas_call | solution.py:323
  (10 shorter events, 0.1 us)
Async XLA Ops:
  0.6 81.7 %copy-start.2 = (s32[1,128,128]{2,1,0:T(8,128)S(1)}, s32[1,128,128]{2,1,0:T(8,128)}, u32[]{:S(2)}) copy-start(s32[1,128,128]{2,1,0:T(8,128)} %param.15) | copy-start | bytes 196612
  5.1 37.9 %collective-permute-start = (f32[5,16,1024]{2,1,0:T(8,128)S(1)}, f32[5,16,1024]{2,1,0:T(8,128)S(1)}, u32[]{:S(2)}, u32[]{:S(2)}) collective-permute-start(f32[5,16,1024]{2,1,0:T(8,128)S(1)} %get-tuple-element.21), channel_id=1, source_target_pairs={{0,120},{8,0},{16,8},{24,16},{32,24},{40,32},{48,40},{56,48},{64,5... | collective-permute-start | bytes 983048 | tf_op jit(solution)/shard_map/ppermute | solution.py:266
  6.6 36.5 %collective-permute-start.1 = (f32[5,16,1024]{2,1,0:T(8,128)S(1)}, f32[5,16,1024]{2,1,0:T(8,128)S(1)}, u32[]{:S(2)}, u32[]{:S(2)}) collective-permute-start(f32[5,16,1024]{2,1,0:T(8,128)S(1)} %get-tuple-element.20), channel_id=1, source_target_pairs={{0,8},{8,16},{16,24},{24,32},{32,40},{40,48},{48,56},{56,64},{64,7... | collective-permute-start | bytes 983048 | tf_op jit(solution)/shard_map/ppermute | solution.py:267
  10.2 17.0 %collective-permute-start.4 = (f32[1,1024]{1,0:T(1,128)S(1)}, f32[1,1024]{1,0:T(1,128)S(1)}, u32[]{:S(2)}, u32[]{:S(2)}) collective-permute-start(f32[1,1024]{1,0:T(1,128)S(1)} %get-tuple-element.7), channel_id=1, source_target_pairs={{9,0},{10,1},{11,2},{12,3},{13,4},{14,5},{15,6},{17,8},{18,9},{19,... | collective-permute-start | bytes 12296 | tf_op jit(solution)/shard_map/ppermute | solution.py:283
  11.5 17.0 %collective-permute-start.5 = (f32[1,1024]{1,0:T(1,128)S(1)}, f32[1,1024]{1,0:T(1,128)S(1)}, u32[]{:S(2)}, u32[]{:S(2)}) collective-permute-start(f32[1,1024]{1,0:T(1,128)S(1)} %get-tuple-element.8), channel_id=1, source_target_pairs={{120,1},{121,2},{122,3},{123,4},{124,5},{125,6},{126,7},{0,9},{1,1... | collective-permute-start | bytes 12296 | tf_op jit(solution)/shard_map/ppermute | solution.py:283
  17.0 16.5 %collective-permute-start.6 = (f32[1,1024]{1,0:T(1,128)S(1)}, f32[1,1024]{1,0:T(1,128)S(1)}, u32[]{:S(2)}, u32[]{:S(2)}) collective-permute-start(f32[1,1024]{1,0:T(1,128)S(1)} %get-tuple-element.9), channel_id=1, source_target_pairs={{8,1},{9,2},{10,3},{11,4},{12,5},{13,6},{14,7},{16,9},{17,10},{18,... | collective-permute-start | bytes 12296 | tf_op jit(solution)/shard_map/ppermute | solution.py:283
  27.2 15.8 %collective-permute-start.2 = (f32[5,8,1024]{2,1,0:T(8,128)S(1)}, f32[5,8,1024]{2,1,0:T(8,128)S(1)}, u32[]{:S(2)}, u32[]{:S(2)}) collective-permute-start(f32[5,8,1024]{2,1,0:T(8,128)S(1)} %constant_dynamic-update-slice_fusion), channel_id=1, source_target_pairs={{1,0},{2,1},{3,2},{4,3},{5,4},{6,5},{7,6},{9,8},{10,9},{11,10},{12... | collective-permute-start | bytes 491528 | tf_op jit(solution)/shard_map/ppermute | solution.py:268
  28.5 14.5 %collective-permute-start.3 = (f32[5,8,1024]{2,1,0:T(8,128)S(1)}, f32[5,8,1024]{2,1,0:T(8,128)S(1)}, u32[]{:S(2)}, u32[]{:S(2)}) collective-permute-start(f32[5,8,1024]{2,1,0:T(8,128)S(1)} %constant_dynamic-update-slice_fusion.5), channel_id=1, source_target_pairs={{0,1},{1,2},{2,3},{3,4},{4,5},{5,6},{6,7},{8,9},{9,10},{10,11},{11... | collective-permute-start | bytes 491528 | tf_op jit(solution)/shard_map/ppermute | solution.py:271
  33.5 9.5 %collective-permute-start.7 = (f32[1,1024]{1,0:T(1,128)S(1)}, f32[1,1024]{1,0:T(1,128)S(1)}, u32[]{:S(2)}, u32[]{:S(2)}) collective-permute-start(f32[1,1024]{1,0:T(1,128)S(1)} %get-tuple-element.6), channel_id=1, source_target_pairs={{121,0},{122,1},{123,2},{124,3},{125,4},{126,5},{127,6},{1,8},{2,9... | collective-permute-start | bytes 12296 | tf_op jit(solution)/shard_map/ppermute | solution.py:283
  43.1 2.4 %copy-start = (bf16[19,8,16,1024]{3,2,1,0:T(8,128)(2,1)S(1)}, bf16[19,8,16,1024]{3,2,1,0:T(8,128)(2,1)}, u32[]{:S(2)}) copy-start(bf16[19,8,16,1024]{3,2,1,0:T(8,128)(2,1)} %saved.1) | copy-start | bytes 14942212
  45.5 1.0 %copy-start.1 = (s32[8,16,1024]{2,1,0:T(8,128)S(1)}, s32[8,16,1024]{2,1,0:T(8,128)}, u32[]{:S(2)}) copy-start(s32[8,16,1024]{2,1,0:T(8,128)} %solid.1) | copy-start | bytes 1572868
  73.9 18.2 %all-to-all-start = ((f32[128,1,128]{2,1,0:T(1,128)}), f32[128,1,128]{2,1,0:T(1,128)S(1)}, u32[]{:S(2)}, u32[]{:S(2)}) async-start(f32[128,1,128]{2,1,0:T(1,128)} %bitcast.30), calls=%async_computation | async-start | bytes 131072 | tf_op jit(solution)/shard_map/all_to_all | solution.py:322

commit v2 on v1

v2 whole, which is shorter than its diff:
```python
import jax
import jax.numpy as jnp
from jax import lax
from jax.experimental import pallas as pl
from jax.experimental.pallas import tpu as pltpu
from jax.sharding import PartitionSpec as P

Q = 19
CS = 8
CV = 16
NX = 1024
CAP = 128
OWNERS = 128
ELEM_DEV = 4096
PAIRS = 9
LANES = 128
COLS = NX // LANES
ROWS = PAIRS * CS * CV * COLS
OMEGA = 1.6

VECS = [
    (0, 0, 0),
    (1, 0, 0),
    (-1, 0, 0),
    (0, 1, 0),
    (0, -1, 0),
    (0, 0, 1),
    (0, 0, -1),
    (1, 1, 0),
    (-1, -1, 0),
    (1, -1, 0),
    (-1, 1, 0),
    (1, 0, 1),
    (-1, 0, -1),
    (1, 0, -1),
    (-1, 0, 1),
    (0, 1, 1),
    (0, -1, -1),
    (0, 1, -1),
    (0, -1, 1),
]
SPAN_UP = [i for i in range(Q) if VECS[i][0] == 1]
SPAN_DOWN = [i for i in range(Q) if VECS[i][0] == -1]
VERT_UP = [i for i in range(Q) if VECS[i][1] == 1]
VERT_DOWN = [i for i in range(Q) if VECS[i][1] == -1]

VMEM = pl.BlockSpec(memory_space=pltpu.VMEM)
SMEM = pl.BlockSpec(memory_space=pltpu.SMEM)
HBM = pl.BlockSpec(memory_space=pltpu.HBM)
SPAN_PAIRS = [p for p in range(PAIRS) if VECS[2 * p + 1][0] != 0]
SIDE_ROWS = 5 * CV * COLS
RIM_ROWS = 2 * SIDE_ROWS + 2 * 5 * CS * COLS
GROUPS = CAP // 8
LISTED = OWNERS * GROUPS
INNER = CS - 2


def collide(pulled, sums, diffs, saved, is_solid, store):
    f = [saved(i) for i in range(Q)]
    e = [None] * PAIRS
    o = [None] * PAIRS
    for p in range(PAIRS):
        e[p] = f[2 * p + 1] + f[2 * p + 2]
        o[p] = f[2 * p + 1] - f[2 * p + 2]
    rho = f[0] + ((e[0] + e[1]) + (e[2] + e[3])) + ((e[4] + e[5]) + (e[6] + e[7]) + e[8])
    us = (o[0] + ((o[3] + o[4]) + (o[5] + o[6]))) / rho
    uv = (o[1] + ((o[3] - o[4]) + (o[7] + o[8]))) / rho
    ux = (o[2] + ((o[5] - o[6]) + (o[7] - o[8]))) / rho
    usq = us * us + uv * uv + ux * ux
    d0, d1, d2, d3, d4, d5, d6, d7, d8 = diffs
    s0, s1, s2, s3, s4, s5, s6, s7, s8 = sums
    w = 1.0 / 36.0
    s34 = s3 + s4
    s56 = s5 + s6
    s78 = s7 + s8
    two0 = 2.0 * s0
    two1 = 2.0 * s1
    two2 = 2.0 * s2
    m0 = 12.0 * pulled[0] + (two0 + two1 + two2) + (s34 + s56 + s78)
    mss = two0 + s34 + s56
    mvv = two1 + s34 + s78
    mxx = two2 + s56 + s78
    msv = s3 - s4
    msx = s5 - s6
    mvx = s7 - s8
    ms = 2.0 * d0 + ((d3 + d4) + (d5 + d6))
    mv = 2.0 * d1 + ((d3 - d4) + (d7 + d8))
    mx = 2.0 * d2 + ((d5 - d6) + (d7 - d8))
    as_ = mss * us + msv * uv + msx * ux
    av = msv * us + mvv * uv + mvx * ux
    ax = msx * us + mvx * uv + mxx * ux
    k = OMEGA * w
    g = (k * m0) * (1.0 + 1.5 * usq) - (4.5 * k) * (us * as_ + uv * av + ux * ax)
    gs = (3.0 * k) * ((ms + 3.0 * as_) - us * m0)
    gv = (3.0 * k) * ((mv + 3.0 * av) - uv * m0)
    gx = (3.0 * k) * ((mx + 3.0 * ax) - ux * m0)
    keep = 1.0 - OMEGA
    store(0, jnp.where(is_solid, pulled[0], keep * pulled[0] + g))
    along = [gs, gv, gx, gs + gv, gs - gv, gs + gx, gs - gx, gv + gx, gv - gx]
    for p in range(PAIRS):
        a = pulled[2 * p + 1]
        b = pulled[2 * p + 2]
        store(2 * p + 1, jnp.where(is_solid, b, keep * a + (g + along[p])))
        store(2 * p + 2, jnp.where(is_solid, a, keep * b + (g - along[p])))


def col(xt):
    return slice(LANES * xt, LANES * (xt + 1))


def vert_shifted(x, rim, cv):
    if cv == 0:
        return x
    vrow = lax.broadcasted_iota(jnp.int32, (CV, LANES), 0)
    shifted = 0.0 if x is None else pltpu.roll(x, CV - 1 if cv == 1 else 1, 0)
    entering = 0.0 if rim is None else jnp.broadcast_to(rim, (CV, LANES))
    return jnp.where(vrow == (CV - 1 if cv == 1 else 0), entering, shifted)


def puller(column):
    lane = lax.broadcasted_iota(jnp.int32, (CV, LANES), 1)
    rolled = {}

    def rolled_column(i, xt):
        if (i, xt) not in rolled:
            rolled[i, xt] = pltpu.roll(column(i, xt), LANES - 1 if VECS[i][2] == 1 else 1, 1)
        return rolled[i, xt]

    def pulled(i, xt):
        cx = VECS[i][2]
        if cx == 0:
            return column(i, xt)
        here = rolled_column(i, xt)
        beside = rolled_column(i, (xt + cx) % COLS)
        return jnp.where(lane == (LANES - 1 if cx == 1 else 0), beside, here)

    return pulled


def ahead(x, dist):
    rows = x.shape[0]
    if dist >= LANES:
        return pltpu.roll(x, rows - dist // LANES, 0)
    lane = lax.broadcasted_iota(jnp.int32, x.shape, 1)
    here = pltpu.roll(x, LANES - dist, 1)
    return jnp.where(lane >= LANES - dist, pltpu.roll(here, rows - 1, 0), here)


def behind(x, dist):
    if dist >= LANES:
        return pltpu.roll(x, dist // LANES, 0)
    lane = lax.broadcasted_iota(jnp.int32, x.shape, 1)
    here = pltpu.roll(x, dist, 1)
    return jnp.where(lane < dist, pltpu.roll(here, 1, 0), here)


def compacted(flag, value, place, look_ahead, look_behind, size):
    count = flag
    dist = 1
    while dist < size:
        count = count + jnp.where(place >= dist, look_behind(count, dist), 0)
        dist *= 2
    item = jnp.where(flag == 1, ((place - (count - 1)) << 16) | (value << 1) | 1, 0)
    dist, bit = 1, 16
    while dist < size:
        other = look_ahead(item, dist)
        stays = jnp.where((item >> bit) & 1 == 0, item, 0)
        item = jnp.where((other >> bit) & 1 == 1, other, stays)
        dist *= 2
        bit += 1
    return (item & 0xFFFF) >> 1, count


def group_list(groups_row):
    shape = (GROUPS, LANES)
    sub = lax.broadcasted_iota(jnp.int32, shape, 0)
    lane = lax.broadcasted_iota(jnp.int32, shape, 1)
    mine = jnp.take_along_axis(jnp.broadcast_to(groups_row, shape), sub * 8 + (lane >> 4), axis=1)
    flag = jnp.where((lane & 15) < mine, 1, 0)
    place = sub * LANES + lane
    return compacted(flag, place, place, ahead, behind, LISTED)


def faces_kernel(adj, hv_up, hv_dn, tiles, sem):
    copies = []
    for k, i in enumerate(VERT_UP):
        copies.append(pltpu.make_async_copy(adj.at[i, :, pl.ds(0, 8)], tiles.at[k], sem.at[k]))
    for k, i in enumerate(VERT_DOWN):
        copies.append(pltpu.make_async_copy(adj.at[i, :, pl.ds(CV - 8, 8)], tiles.at[5 + k], sem.at[5 + k]))
    for c in copies:
        c.start()
    for k in range(10):
        copies[k].wait()
        for s in range(CS):
            if k < 5:
                hv_up[k, s : s + 1, :] = tiles[k, s, 0:1, :]
            else:
                hv_dn[k - 5, s : s + 1, :] = tiles[k, s, 7:8, :]


CHUNKS = 4
STEP = CS // CHUNKS
N_LOAD = 13


def load_copies(adj, wide, sem, q, lo, hi, first):
    copies = []
    for a, b in ((0, 1), (3, 7), (15, 19)):
        pops = pl.ds(a, b - a)
        copies.append((adj.at[pops, pl.ds(lo, hi - lo)], wide.at[pops, pl.ds(lo - first, hi - lo)]))
    for i in SPAN_UP:
        n = min(hi, CS - 1) - lo
        if n > 0:
            copies.append((adj.at[i, pl.ds(lo + 1, n)], wide.at[i, pl.ds(lo - first, n)]))
    for i in SPAN_DOWN:
        at = max(lo, 1)
        if hi > at:
            copies.append((adj.at[i, pl.ds(at - 1, hi - at)], wide.at[i, pl.ds(at - first, hi - at)]))
    return [pltpu.make_async_copy(a, b, sem.at[q, k]) for k, (a, b) in enumerate(copies)]


def tables_kernel(
    cells_ref, dirs_ref, weight_ref, counts_ref, adj,
    table, hs_up, hs_dn, ridx, hidx, lidx, pos, weight, list_a, list_b,
    wide, tilted, load_sem, face_sem,
):
    copies = [load_copies(adj, wide, load_sem, q, STEP * q, STEP * (q + 1), 0) for q in range(CHUNKS)]
    faces = []
    tilts = []
    for k in range(5):
        for i, s, out in ((SPAN_UP[k], 0, hs_up), (SPAN_DOWN[k], CS - 1, hs_dn)):
            dest = out.at[k]
            if VECS[i][1] != 0:
                tilts.append((len(tilts), VECS[i][1], out, k))
                dest = tilted.at[tilts[-1][0]]
            faces.append(pltpu.make_async_copy(adj.at[i, s], dest, face_sem.at[len(faces)]))
    for c in sum(copies, []) + faces:
        c.start()
    zero = jnp.zeros((CV, NX), jnp.float32)
    for i in SPAN_UP:
        wide[i, CS - 1] = zero
    for i in SPAN_DOWN:
        wide[i, 0] = zero

    cells = cells_ref[...]
    dirs = dirs_ref[...]
    pair = (dirs - 1) >> 1
    xc = (cells >> 7) & 7
    v = (cells >> 10) & 15
    s = cells >> 14
    in_slab = (v >> 3) * 64 + xc * 8 + (v & 7)
    ridx[...] = pair * 1024 + s * 128 + in_slab
    lidx[...] = cells & 127
    lane = lax.broadcasted_iota(jnp.int32, (OWNERS, CAP), 1)
    counts = jnp.broadcast_to(counts_ref[...].astype(jnp.float32), (OWNERS, OWNERS))
    live = lane.astype(jnp.float32) < jnp.transpose(counts)
    signed = jnp.where((dirs & 1) == 1, weight_ref[...], -weight_ref[...])
    weight[...] = jnp.where(live, signed, 0.0)
    has_s = (pair == 0) | ((pair >= 3) & (pair <= 6))
    k_s = jnp.where(pair == 0, 0, pair - 2)
    has_v = (pair == 1) | (pair == 3) | (pair == 4) | (pair >= 7)
    k_v = jnp.where(pair == 1, 0, jnp.where(pair < 7, pair - 2, pair - 4))
    on_s = has_s & ((s == 0) | (s == CS - 1))
    on_v = has_v & ((v == 0) | (v == CV - 1))
    at_s = (jnp.where(s == 0, 0, 5) + k_s) * 128 + in_slab
    at_v = 2 * SIDE_ROWS + ((jnp.where(v == 0, 0, 5) + k_v) * 8 + xc) * 8 + s
    flag = jnp.where(live & (on_s | on_v), 1, 0)
    where_rim = jnp.where(on_s, at_s, at_v)
    rows, count = compacted(
        flag, where_rim, lane,
        lambda x, d: pltpu.roll(x, CAP - d, 1), lambda x, d: pltpu.roll(x, d, 1), CAP,
    )
    hidx[...] = rows
    pos[...] = jnp.where(flag == 1, count - 1, -1)
    totals = jnp.transpose(count.astype(jnp.float32))[CAP - 1 : CAP, :].astype(jnp.int32)
    for out, groups in ((list_a, (counts_ref[...] + 7) >> 3), (list_b, (totals + 7) >> 3)):
        ids, running = group_list(groups)
        out[0:GROUPS, :] = ids
        out[GROUPS : 2 * GROUPS, :] = running
    list_b[2 * GROUPS : 2 * GROUPS + 8, :] = jnp.broadcast_to(jnp.max(totals, axis=1, keepdims=True), (8, LANES))
    list_a[2 * GROUPS : 2 * GROUPS + 8, :] = jnp.zeros((8, LANES), jnp.int32)

    def slab(s, carry):
        def column(i, xt):
            return vert_shifted(wide[i, s, :, col(xt)], None, VECS[i][1])

        pulled = puller(column)
        for xt in range(COLS):
            for p in range(PAIRS):
                diff = pulled(2 * p + 1, xt) - pulled(2 * p + 2, xt)
                for vt in range(2):
                    at = pl.multiple_of(s * 128 + (p * 1024 + 64 * vt + 8 * xt), 8)
                    table[pl.ds(at, 8), :] = diff[8 * vt : 8 * vt + 8]
        return carry

    for q in range(CHUNKS):
        for c in copies[q]:
            c.wait()
        lax.fori_loop(STEP * q, STEP * (q + 1), slab, 0)
    for c in faces:
        c.wait()
    for n, cv, out, k in tilts:
        for xt in range(COLS):
            out[k, :, col(xt)] = vert_shifted(tilted[n, :, col(xt)], None, cv)


PER_TURN = 32


def pick(group, index, table, lidx, picked):
    sub = lax.broadcasted_iota(jnp.int32, (8, LANES), 0)
    first = group * 8
    v = jnp.broadcast_to(table[pl.ds(index[first], 1), :], (8, LANES))
    for j in range(1, 8):
        row = table[pl.ds(index[first + j], 1), :]
        v = jnp.where(sub == j, jnp.broadcast_to(row, (8, LANES)), v)
    lrow = jnp.broadcast_to(lidx[pl.ds(group >> 4, 1), :], (8, LANES))
    picked[group] = jnp.take_along_axis(v, lrow, axis=1)


def pick_rest(start, listed, index, table, lidx, picked):
    total = listed[2 * LISTED - 1]

    def turn(m, carry):
        for q in range(PER_TURN):
            pick(listed[m * PER_TURN + q], index, table, lidx, picked)
        return carry

    lax.fori_loop(start // PER_TURN, (total + PER_TURN - 1) // PER_TURN, turn, 0)


def fill_rims(v_up, v_dn, vup, vdn):
    for halo, rims in ((v_up, vup), (v_dn, vdn)):
        for k in range(5):
            for xt in range(COLS):
                rims[k, xt] = halo[k, :, col(xt)]


def collide_column(pull, xt, sav, sol, obuf, s):
    pulled = [pull(i, xt) for i in range(Q)]
    sums = [pulled[2 * p + 1] + pulled[2 * p + 2] for p in range(PAIRS)]
    diffs = [pulled[2 * p + 1] - pulled[2 * p + 2] for p in range(PAIRS)]

    def store(i, v):
        obuf[i, s, :, col(xt)] = v

    collide(
        pulled, sums, diffs,
        lambda i: sav[i, s, :, col(xt)].astype(jnp.float32),
        sol[s, :, col(xt)] == 1,
        store,
    )


BESIDE = 24
IN_CHUNKS = 3
IN_STEP = INNER // IN_CHUNKS


def inner_kernel(
    index, listed, lidx, table, v_up, v_dn, adj, saved, solid,
    out, local, picked, wide, sav, sol, obuf, vup, vdn, load_sem, misc_sem, out_sem,
):
    copies = []
    for q in range(IN_CHUNKS):
        lo = 1 + IN_STEP * q
        copies.append(load_copies(adj, wide, load_sem, q, lo, lo + IN_STEP, 1))
        mine = pl.ds(IN_STEP * q, IN_STEP)
        copies[q].append(pltpu.make_async_copy(saved.at[:, pl.ds(lo, IN_STEP)], sav.at[:, mine], misc_sem.at[q, 0]))
        copies[q].append(pltpu.make_async_copy(solid.at[pl.ds(lo, IN_STEP)], sol.at[mine], misc_sem.at[q, 1]))
        for c in copies[q]:
            c.start()
    fill_rims(v_up, v_dn, vup, vdn)

    def slab(n, carry):
        def column(i, xt):
            cs, cv, _ = VECS[i]
            rim = None
            if cv != 0:
                src, own = (vup, VERT_UP) if cv == 1 else (vdn, VERT_DOWN)
                rim = src[own.index(i), xt, pl.ds(n + 1 + cs, 1), :]
            return vert_shifted(wide[i, n, :, col(xt)], rim, cv)

        pull = puller(column)
        for xt in range(COLS):
            collide_column(pull, xt, sav, sol, obuf, n)
            for q in range(BESIDE):
                pick(listed[(n * COLS + xt) * BESIDE + q], index, table, lidx, picked)
        pltpu.make_async_copy(obuf.at[:, n], out.at[:, n + 1], out_sem.at[n]).start()
        return carry

    for q in range(IN_CHUNKS):
        for c in copies[q]:
            c.wait()
        lax.fori_loop(IN_STEP * q, IN_STEP * (q + 1), slab, 0)
    pick_rest(INNER * COLS * BESIDE, listed, index, table, lidx, picked)
    sub = lax.broadcasted_iota(jnp.int32, (8, LANES), 0)
    lane = lax.broadcasted_iota(jnp.int32, (8, LANES), 1)

    def turn(b, carry):
        for q in range(8):
            t = b * 8 + q
            acc = picked[t * GROUPS]
            for g in range(1, GROUPS):
                acc = jnp.where((lane >> 3) == g, picked[t * GROUPS + g], acc)
            acc = jnp.where((lane & 7) == sub, acc, 0.0)
            local[pl.ds(t, 1), :] = jnp.sum(acc, axis=0, keepdims=True)
        return carry

    lax.fori_loop(0, OWNERS // 8, turn, 0)
    for n in range(INNER):
        pltpu.make_async_copy(obuf.at[:, n], out.at[:, n + 1], out_sem.at[n]).wait()


FIRST = 6


def rim_kernel(
    index, listed, lidx, pos, weight, local, h_up, h_dn, v_up, v_dn, values, rim, picked,
):
    for side, s, halo, pops in ((0, 0, h_dn, SPAN_DOWN), (1, CS - 1, h_up, SPAN_UP)):
        def column(i, xt):
            cs, cv, _ = VECS[i]
            if i in pops:
                return halo[pops.index(i), :, col(xt)]
            src, own = (v_up, VERT_UP) if cv == 1 else (v_dn, VERT_DOWN)
            return vert_shifted(None, src[own.index(i), s + cs : s + cs + 1, col(xt)], cv)

        pulled = puller(column)
        for k, p in enumerate(SPAN_PAIRS):
            plus, minus = 2 * p + 1, 2 * p + 2
            for xt in range(COLS):
                if VECS[plus][1] != 0:
                    d = pulled(plus, xt) - pulled(minus, xt)
                else:
                    d = pulled(plus, xt) if plus in pops else -pulled(minus, xt)
                for vt in range(2):
                    at = (side * 5 + k) * 128 + 64 * vt + 8 * xt
                    rim[at : at + 8, :] = d[8 * vt : 8 * vt + 8]
    lane = lax.broadcasted_iota(jnp.int32, (8, LANES), 1)
    sub = lax.broadcasted_iota(jnp.int32, (8, LANES), 0)
    for side, halo, pops in ((0, v_dn, VERT_DOWN), (1, v_up, VERT_UP)):
        for k, i in enumerate(pops):
            cs, _, cx = VECS[i]
            cols = [halo[k, :, col(xt)] for xt in range(COLS)]
            if cs != 0:
                cols = [pltpu.roll(c, CS - 1 if cs == 1 else 1, 0) for c in cols]
            if cx != 0:
                rolled = [pltpu.roll(c, LANES - 1 if cx == 1 else 1, 1) for c in cols]
                edge = LANES - 1 if cx == 1 else 0
                cols = [jnp.where(lane == edge, rolled[(xt + cx) % COLS], rolled[xt]) for xt in range(COLS)]
            for xt in range(COLS):
                at = 2 * SIDE_ROWS + ((side * 5 + k) * 8 + xt) * 8
                rim[at : at + 8, :] = cols[xt] if i % 2 == 1 else -cols[xt]

    pick_rest(0, listed, index, rim, lidx, picked)
    most = listed[2 * LISTED]

    def added(t, groups):
        posb = jnp.broadcast_to(pos[pl.ds(t, 1), :], (8, LANES))
        acc = jnp.zeros((8, LANES), jnp.float32)
        for g in groups:
            acc = acc + jnp.where(posb == sub + 8 * g, picked[t * GROUPS + g], 0.0)
        return jnp.sum(acc, axis=0, keepdims=True)

    def turn(b, carry):
        for q in range(8):
            t = b * 8 + q
            w = weight[pl.ds(t, 1), :]
            total = local[pl.ds(t, 1), :] + added(t, range(FIRST))
            values[pl.ds(t, 1), :] = jnp.where(w == 0.0, 0.0, w * total)
        return carry

    lax.fori_loop(0, OWNERS // 8, turn, 0)

    @pl.when(most > 8 * FIRST)
    def _():
        def more(t, carry):
            w = weight[pl.ds(t, 1), :]
            rest = w * added(t, range(FIRST, GROUPS))
            values[pl.ds(t, 1), :] = values[pl.ds(t, 1), :] + jnp.where(w == 0.0, 0.0, rest)
            return carry

        lax.fori_loop(0, OWNERS, more, 0)


def outer_kernel(
    h_up, h_dn, v_up, v_dn, adj, saved, solid, partial, out, wide, sav, sol, obuf, load_sem, out_sem,
):
    del partial
    ends = ((0, 0, h_dn, SPAN_DOWN), (1, CS - 1, h_up, SPAN_UP))
    copies = []
    for n, s, halo, pops in ends:
        moves = [
            (adj.at[pl.ds(a, b - a), s], wide.at[pl.ds(a, b - a), n]) for a, b in ((0, 1), (3, 7), (15, 19))
        ]
        for i in SPAN_UP + SPAN_DOWN:
            if i not in pops:
                moves.append((adj.at[i, s + VECS[i][0]], wide.at[i, n]))
        moves.append((saved.at[:, s], sav.at[:, n]))
        moves.append((solid.at[s], sol.at[n]))
        copies.append([pltpu.make_async_copy(a, b, load_sem.at[n, k]) for k, (a, b) in enumerate(moves)])
        for c in copies[n]:
            c.start()
    for n, s, halo, pops in ends:
        for c in copies[n]:
            c.wait()

        def column(i, xt):
            cs, cv, _ = VECS[i]
            if i in pops:
                return halo[pops.index(i), :, col(xt)]
            rim = None
            if cv != 0:
                src, own = (v_up, VERT_UP) if cv == 1 else (v_dn, VERT_DOWN)
                rim = src[own.index(i), s + cs : s + cs + 1, col(xt)]
            return vert_shifted(wide[i, n, :, col(xt)], rim, cv)

        pull = puller(column)
        for xt in range(COLS):
            collide_column(pull, xt, sav, sol, obuf, n)
        pltpu.make_async_copy(obuf.at[:, n], out.at[:, s], out_sem.at[n]).start()
    for n, s, halo, pops in ends:
        pltpu.make_async_copy(obuf.at[:, n], out.at[:, s], out_sem.at[n]).wait()


def sums_kernel(slots, received, out):
    his = ELEM_DEV // LANES
    sub_lo = lax.broadcasted_iota(jnp.int32, (LANES, 2 * LANES), 0)
    sub_hi = lax.broadcasted_iota(jnp.int32, (his, 2 * LANES), 0)

    def turn(t, acc):
        for q in range(8):
            r = (t * 8 + q) * 2
            slot = jnp.concatenate([slots[pl.ds(r, 1), :], slots[pl.ds(r + 1, 1), :]], 1)
            v0 = jnp.concatenate([received[r], received[r + 1]], 1)
            a = v0.astype(jnp.bfloat16).astype(jnp.float32)
            b = (v0 - a).astype(jnp.bfloat16).astype(jnp.float32)
            c = (v0 - a) - b
            hit = jnp.broadcast_to(slot >> 7, (his, 2 * LANES)) == sub_hi
            left = jnp.concatenate(
                [jnp.where(hit, jnp.broadcast_to(v, (his, 2 * LANES)), 0.0).astype(jnp.bfloat16) for v in (a, b, c)], 0
            )
            right = jnp.where(jnp.broadcast_to(slot & 127, (LANES, 2 * LANES)) == sub_lo, 1.0, 0.0).astype(jnp.bfloat16)
            acc = acc + lax.dot_general(
                left, right, (((1,), (1,)), ((), ())), preferred_element_type=jnp.float32
            )
        return acc

    acc = lax.fori_loop(0, OWNERS // 16, turn, jnp.zeros((3 * his, LANES), jnp.float32))
    out[...] = acc[0:his] + acc[his : 2 * his] + acc[2 * his : 3 * his]


def cost(us):
    return pl.CostEstimate(flops=0, bytes_accessed=int(us * 3.0e6), transcendentals=0)


def limit(mib):
    return pltpu.CompilerParams(vmem_limit_bytes=mib << 20)


F32 = jnp.float32
I32 = jnp.int32
GRID = (OWNERS, CAP)


def shape(dims, kind=F32):
    return jax.ShapeDtypeStruct(dims, kind)


def faces_call(adjoint):
    return pl.pallas_call(
        faces_kernel,
        out_shape=(shape((5, CS, NX)), shape((5, CS, NX))),
        in_specs=[HBM],
        out_specs=(VMEM, VMEM),
        scratch_shapes=[pltpu.VMEM((10, CS, 8, NX), F32), pltpu.SemaphoreType.DMA((10,))],
        compiler_params=limit(56),
        cost_estimate=cost(2),
        name="faces",
    )(adjoint)


def tables_call(cells, dirs, weight, counts, adjoint):
    return pl.pallas_call(
        tables_kernel,
        out_shape=(
            shape((ROWS, LANES)), shape((5, CV, NX)), shape((5, CV, NX)),
            shape(GRID, I32), shape(GRID, I32), shape(GRID, I32), shape(GRID, I32), shape(GRID),
            shape((40, LANES), I32), shape((40, LANES), I32),
        ),
        in_specs=[VMEM] * 4 + [HBM],
        out_specs=(VMEM,) * 10,
        scratch_shapes=[
            pltpu.VMEM((Q, CS, CV, NX), F32),
            pltpu.VMEM((4, CV, NX), F32),
            pltpu.SemaphoreType.DMA((CHUNKS, N_LOAD)),
            pltpu.SemaphoreType.DMA((10,)),
        ],
        compiler_params=limit(50),
        cost_estimate=cost(8),
        name="tables",
    )(cells, dirs, weight, counts, adjoint)


def inner_call(ridx, list_a, lidx, table, v_up, v_dn, adjoint, saved, solid):
    return pl.pallas_call(
        inner_kernel,
        out_shape=(shape((Q, CS, CV, NX)), shape(GRID)),
        in_specs=[SMEM, SMEM] + [VMEM] * 4 + [HBM] * 3,
        out_specs=(HBM, VMEM),
        scratch_shapes=[
            pltpu.VMEM((LISTED, 8, LANES), F32),
            pltpu.VMEM((Q, INNER, CV, NX), F32),
            pltpu.VMEM((Q, INNER, CV, NX), jnp.bfloat16),
            pltpu.VMEM((INNER, CV, NX), I32),
            pltpu.VMEM((Q, INNER, CV, NX), F32),
            pltpu.VMEM((5, COLS, CS, LANES), F32),
            pltpu.VMEM((5, COLS, CS, LANES), F32),
            pltpu.SemaphoreType.DMA((IN_CHUNKS, N_LOAD)),
            pltpu.SemaphoreType.DMA((IN_CHUNKS, 2)),
            pltpu.SemaphoreType.DMA((INNER,)),
        ],
        compiler_params=limit(50),
        cost_estimate=cost(15),
        name="inner",
    )(ridx.reshape(-1), list_a.reshape(-1), lidx, table, v_up, v_dn, adjoint, saved, solid)


def rim_call(hidx, list_b, lidx, pos, weight, local, h_up, h_dn, v_up, v_dn):
    return pl.pallas_call(
        rim_kernel,
        out_shape=shape(GRID),
        in_specs=[SMEM, SMEM] + [VMEM] * 8,
        out_specs=VMEM,
        scratch_shapes=[pltpu.VMEM((RIM_ROWS, LANES), F32), pltpu.VMEM((LISTED, 8, LANES), F32)],
        compiler_params=limit(50),
        cost_estimate=cost(5),
        name="rim",
    )(hidx.reshape(-1), list_b.reshape(-1), lidx, pos, weight, local, h_up, h_dn, v_up, v_dn)


def outer_call(h_up, h_dn, v_up, v_dn, adjoint, saved, solid, partial):
    return pl.pallas_call(
        outer_kernel,
        out_shape=shape((Q, CS, CV, NX)),
        in_specs=[VMEM] * 4 + [HBM] * 4,
        out_specs=HBM,
        scratch_shapes=[
            pltpu.VMEM((Q, 2, CV, NX), F32),
            pltpu.VMEM((Q, 2, CV, NX), jnp.bfloat16),
            pltpu.VMEM((2, CV, NX), I32),
            pltpu.VMEM((Q, 2, CV, NX), F32),
            pltpu.SemaphoreType.DMA((2, 10)),
            pltpu.SemaphoreType.DMA((2,)),
        ],
        input_output_aliases={7: 0},
        compiler_params=limit(56),
        cost_estimate=cost(3),
        name="outer",
    )(h_up, h_dn, v_up, v_dn, adjoint, saved, solid, partial)


def sums_call(slots, received):
    return pl.pallas_call(
        sums_kernel,
        out_shape=shape((ELEM_DEV // LANES, LANES)),
        in_specs=[VMEM, VMEM],
        out_specs=VMEM,
        cost_estimate=cost(4),
        name="element_sums",
    )(slots, received)


def body(adjoint, saved, solid, send_cells, send_dirs, send_weight, send_counts, recv_slots):
    ns = lax.axis_size("span")
    nv = lax.axis_size("vert")
    hv_up, hv_dn = faces_call(adjoint)
    v_up = lax.ppermute(hv_up, "vert", [(i, i - 1) for i in range(1, nv)])
    v_dn = lax.ppermute(hv_dn, "vert", [(i, i + 1) for i in range(nv - 1)])
    table, hs_up, hs_dn, ridx, hidx, lidx, pos, weight, list_a, list_b = tables_call(
        send_cells[0], send_dirs[0], send_weight[0], send_counts, adjoint
    )
    hs_up = hs_up.at[1, CV - 1].set(v_up[1, 0]).at[2, 0].set(v_dn[2, 0])
    hs_dn = hs_dn.at[1, 0].set(v_dn[1, CS - 1]).at[2, CV - 1].set(v_up[2, CS - 1])
    hs_up, hs_dn, list_a = lax.optimization_barrier((hs_up, hs_dn, list_a))
    h_up = lax.ppermute(hs_up, "span", [(i, (i - 1) % ns) for i in range(ns)])
    h_dn = lax.ppermute(hs_dn, "span", [(i, (i + 1) % ns) for i in range(ns)])
    partial, local = inner_call(ridx, list_a, lidx, table, v_up, v_dn, adjoint, saved, solid)
    values = rim_call(hidx, list_b, lidx, pos, weight, local, h_up, h_dn, v_up, v_dn)
    values, v_up, v_dn = lax.optimization_barrier((values, v_up, v_dn))
    received = lax.all_to_all(values[:, None, :], ("span", "vert"), split_axis=0, concat_axis=0, tiled=True)
    adjoint_prev = outer_call(h_up, h_dn, v_up, v_dn, adjoint, saved, solid, partial)
    sens = sums_call(recv_slots[0], received)
    return adjoint_prev, sens.reshape(ELEM_DEV)


def solution(mesh):
    return jax.shard_map(
        body,
        mesh=mesh,
        in_specs=(
            P(None, "span", "vert", None),
            P(None, "span", "vert", None),
            P("span", "vert", None),
            P(("span", "vert"), None, None),
            P(("span", "vert"), None, None),
            P(("span", "vert"), None, None),
            P(("span", "vert"), None),
            P(("span", "vert"), None, None),
        ),
        out_specs=(P(None, "span", "vert", None), P(("span", "vert"))),
        check_vma=False,
    )
```

time: 100 us -> 77.3 us (0.77)
  Pallas kernels: 32.5 us -> 48.3 us
  starting transfers between devices: 34.2 us -> 22 us
  waiting for transfers between devices: 16.3 us -> 4.55 us
  local copies, waits for them, and re-layouts: 12.6 us -> 1.1 us
  other arithmetic: 2.67 us -> 0 us
    ppermute x8 -> x4, starting transfers between devices: 25.7 us -> 8.69 us  [the longest x1 3.95 us: body(): v_dn = lax.ppermute(hv_dn, 'vert', [(i, i + 1) for i in range(nv - 1)])]
    pallas_call x2 -> x6, Pallas kernels: 32.5 us -> 48.3 us  [the longest x1 21.2 us: inner_call(): pl.pallas_call(inner_kernel, out_shape=(shape((Q, CS, CV, NX)), shape(GRI...]
    ppermute x8 -> x4, waiting for transfers between devices: 7.29 us -> 0.01 us  [the longest x1 0.01 us: body(): v_dn = lax.ppermute(hv_dn, 'vert', [(i, i + 1) for i in range(nv - 1)])]
    unnamed x18 -> x20, local copies, waits for them, and re-layouts: 7.09 us -> 0.65 us
    all_to_all x1, starting transfers between devices: 8.49 us -> 13.4 us  [body(): lax.all_to_all(values[:, None, :], ('span', 'vert'), split_axis=0, concat...]
    all_to_all x1, waiting for transfers between devices: 9.04 us -> 4.54 us  [body(): lax.all_to_all(values[:, None, :], ('span', 'vert'), split_axis=0, concat...]
    another operation x5 -> x0, local copies, waits for them, and re-layouts: 2.37 us -> none  [the longest x1 0.89 us: halos(): jnp.stack([adjoint[i, CS - 1] for i in SPAN_DOWN], 0)]
    slice x1 -> x2, local copies, waits for them, and re-layouts: 1.99 us -> 0.02 us  [the longest x1 0.01 us: body(): v_up[2, CS - 1]]
  transfers between devices with their start and end apart: 9 -> 5, of which waited for: 2 -> 1; matrix products, arithmetic and copies ran while one was open for 5% -> 0% of each run, Pallas kernels for 0% -> 45%
where the time goes in v2:
time: 77.3 us; the launch traced here: 77 us
  Pallas kernels  48.3 us (62%)
  starting transfers between devices  22 us (28%)
  waiting for transfers between devices  4.55 us (6%)
  local copies, waits for them, and re-layouts  1.1 us (1%)
  between operations  0.9 us (1%)
    pallas_call x1, Pallas kernels, inner_call(): pl.pallas_call(inner_kernel, out_shape=(shape((Q, CS, CV, NX)), shape(GRI...  21.2 us
    all_to_all x1, starting transfers between devices, body(): lax.all_to_all(values[:, None, :], ('span', 'vert'), split_axis=0, concat...  13.4 us
    pallas_call x1, Pallas kernels, tables_call(): pl.pallas_call(tables_kernel, out_shape=(shape((ROWS, LANES)), shape((5,...  8.25 us
    pallas_call x1, Pallas kernels, rim_call(): pl.pallas_call(rim_kernel, out_shape=shape(GRID), in_specs=[SMEM, SMEM] +...  7.22 us
    pallas_call x1, Pallas kernels, outer_call(): pl.pallas_call(outer_kernel, out_shape=shape((Q, CS, CV, NX)), in_specs=[...  5.13 us
    all_to_all x1, waiting for transfers between devices, body(): lax.all_to_all(values[:, None, :], ('span', 'vert'), split_axis=0, concat...  4.54 us
    pallas_call x1, Pallas kernels, sums_call(): pl.pallas_call(sums_kernel, out_shape=shape((ELEM_DEV // LANES, LANES)),...  3.98 us
    ppermute x1, starting transfers between devices, body(): v_dn = lax.ppermute(hv_dn, 'vert', [(i, i + 1) for i in range(nv - 1)])  3.95 us
  transfers between devices with their start and end apart: 5, of which 1 were waited for; matrix products, arithmetic and copies ran while one was open for 0% of the time, Pallas kernels for 45%

profile of v2, /device:TPU:1, one launch (start us, length us, event | category | flops | bytes accessed | tf_op | source)
XLA Modules:
  0.0 77.0 jit_solution(11965289839616485734)
XLA Ops:
  0.6 0.0 copy-start.8
  0.6 0.0 copy-start.7
  0.7 0.0 copy-start.6
  0.7 0.0 copy-start.5
  0.7 0.0 copy-start
  0.7 2.5 %faces.1 = (f32[5,8,1024]{2,1,0:T(8,128)}, f32[5,8,1024]{2,1,0:T(8,128)}) custom-call(f32[19,8,16,1024]{3,2,1,0:T(8,128)} %adj.7), custom_call_target="tpu_custom_call" | custom-call | bytes 6000000 | tf_op jit(solution)/shard_map/faces/pallas_call | solution.py:572
  3.2 4.0 %collective-permute-start.1 = (f32[5,8,1024]{2,1,0:T(8,128)}, f32[5,8,1024]{2,1,0:T(8,128)S(1)}, u32[]{:S(2)}, u32[]{:S(2)}) collective-permute-start(f32[5,8,1024]{2,1,0:T(8,128)} %get-tuple-element.72), channel_id=1, source_target_pairs={{0,1},{1,2},{2,3},{3,4},{4,5},{5,6},{6,7},{8,9},{9,10},{10,11},{11... | collective-permute-start | bytes 491528 | tf_op jit(solution)/shard_map/ppermute | solution.py:680
  7.2 1.3 %collective-permute-start = (f32[5,8,1024]{2,1,0:T(8,128)}, f32[5,8,1024]{2,1,0:T(8,128)S(1)}, u32[]{:S(2)}, u32[]{:S(2)}) collective-permute-start(f32[5,8,1024]{2,1,0:T(8,128)} %get-tuple-element.71), channel_id=1, source_target_pairs={{1,0},{2,1},{3,2},{4,3},{5,4},{6,5},{7,6},{9,8},{10,9},{11,10},{12... | collective-permute-start | bytes 491528 | tf_op jit(solution)/shard_map/ppermute | solution.py:679
  8.5 0.0 copy-done.8
  8.5 0.0 copy-done.7
  8.5 0.0 copy-done.6
  8.5 0.0 copy-done.5
  8.5 8.2 %tables.1 = (f32[9216,128]{1,0:T(8,128)}, f32[5,16,1024]{2,1,0:T(8,128)S(1)}, f32[5,16,1024]{2,1,0:T(8,128)S(1)}, s32[128,128]{1,0:T(8,128)S(1)}, s32[128,128]{1...) custom-call(s32[128,128]{1,0:T(8,128)S(1)} %bitcast.10, ...), custom_call_target="tpu_custom_call" | custom-call | bytes 24000000 | tf_op jit(solution)/shard_map/tables/pallas_call | solution.py:585
  16.8 0.0 collective-permute-done.1.v_dn
  16.8 0.0 copy-start.1
  16.8 0.1 scatter.16
  16.9 0.0 collective-permute-done.v_up
  17.0 0.0 copy-start.2
  17.0 0.1 scatter.14
  17.1 0.1 scatter.19
  17.2 0.1 scatter.15
  17.3 1.0 %collective-permute-start.2 = (f32[5,16,1024]{2,1,0:T(8,128)S(1)}, f32[5,16,1024]{2,1,0:T(8,128)S(1)}, u32[]{:S(2)}, u32[]{:S(2)}) collective-permute-start(f32[5,16,1024]{2,1,0:T(8,128)S(1)} %scatter.15), channel_id=1, source_target_pairs={{0,120},{8,0},{16,8},{24,16},{32,24},{40,32},{48,40},{56,48},{64,5... | collective-permute-start | bytes 983048 | tf_op jit(solution)/shard_map/ppermute | solution.py:687
  18.4 2.4 %collective-permute-start.3 = (f32[5,16,1024]{2,1,0:T(8,128)S(1)}, f32[5,16,1024]{2,1,0:T(8,128)S(1)}, u32[]{:S(2)}, u32[]{:S(2)}) collective-permute-start(f32[5,16,1024]{2,1,0:T(8,128)S(1)} %scatter.19), channel_id=1, source_target_pairs={{0,8},{8,16},{16,24},{24,32},{32,40},{40,48},{48,56},{56,64},{64,7... | collective-permute-start | bytes 983048 | tf_op jit(solution)/shard_map/ppermute | solution.py:688
  20.8 0.0 copy-done
  20.8 21.2 %inner.1 = (f32[19,8,16,1024]{3,2,1,0:T(8,128)}, f32[128,128]{1,0:T(8,128)S(1)}) custom-call(s32[16384]{0:T(1024)S(1)} %bitcast.13, s32[5120]{0:T(1024)S(1)} %bitcast.15, s32[128,128]{1,0:T(8,128)S(1)} %get-tuple-element.79.lidx, f32[9216,128]{1,0:T(8,128)} %get-tuple-element.84.table, f32[5,8,1024]{2,1,0:T(8,128)S(1)} %collective-permute-done.v_up, ...), custom_call_target="tpu_custom_call" | custom-call | bytes 45000000 | tf_op jit(solution)/shard_map/inner/pallas_call | solution.py:607
  42.0 0.0 collective-permute-done.2.h_up
  42.0 0.0 copy-start.3
  42.0 0.0 collective-permute-done.3.h_dn
  42.0 0.0 copy-start.4
  42.1 0.0 copy-done.1
  42.1 0.0 copy-done.2
  42.1 7.2 %rim.1 = f32[128,128]{1,0:T(8,128)} custom-call(s32[16384]{0:T(1024)S(1)} %bitcast.14, s32[5120]{0:T(1024)S(1)} %bitcast.16, s32[128,128]{1,0:T(8,128)S(1)} %get-tuple-element.79.lidx, s32[128,128]{1,0:T(8,128)S(1)} %get-tuple-element.80.pos, f32[128,128]{1,0:T(8,128)S(1)} %get-tuple-element.81.weight, f32[128,128]{1,0:T(8,128)S(1)} %get-tuple-element.85.local, ...), custom_call_target="tpu_custom_call" | custom-call | bytes 15000000 | tf_op jit(solution)/shard_map/rim/pallas_call | solution.py:631
  49.3 13.4 %all-to-all-start = ((f32[128,1,128]{2,1,0:T(1,128)}), f32[128,1,128]{2,1,0:T(1,128)S(1)}, u32[]{:S(2)}, u32[]{:S(2)}) async-start(f32[128,1,128]{2,1,0:T(1,128)} %bitcast.8), calls=%async_computation | async-start | bytes 131072 | tf_op jit(solution)/shard_map/all_to_all | solution.py:692
  62.7 0.0 copy-done.3
  62.7 0.0 copy-done.4
  62.7 5.1 %outer.1 = f32[19,8,16,1024]{3,2,1,0:T(8,128)} custom-call(f32[5,16,1024]{2,1,0:T(8,128)} %copy-done.3, f32[5,16,1024]{2,1,0:T(8,128)} %copy-done.4, f32[5,8,1024]{2,1,0:T(8,128)} %copy-done.2, f32[5,8,1024]{2,1,0:T(8,128)} %copy-done.1, f32[19,8,16,1024]{3,2,1,0:T(8,128)} %adj.7, bf16[19,8,16,1024]{3,2,1,0:T(8,128)(2,1)} %saved.3, ...), custom_call_target="tpu_custom_call", output_to_operand_aliasing={{}: (7, {})} | custom-call | bytes 9000000 | tf_op jit(solution)/shard_map/outer/pallas_call | solution.py:644
  67.8 4.5 %all-to-all-done.received = f32[128,1,128]{2,1,0:T(1,128)S(1)} async-done(((f32[128,1,128]{2,1,0:T(1,128)}), f32[128,1,128]{2,1,0:T(1,128)S(1)}, u32[]{:S(2)}, u32[]{:S(2)}) %all-to-all-start) | async-done | bytes 65568 | tf_op jit(solution)/shard_map/all_to_all | solution.py:692
  72.4 0.0 copy-start.9
  72.4 0.6 copy-done.9
  73.0 4.0 %element_sums.1 = f32[32,128]{1,0:T(8,128)} custom-call(s32[128,128]{1,0:T(8,128)} %bitcast.17, f32[128,1,128]{2,1,0:T(1,128)} %copy-done.9), custom_call_target="tpu_custom_call" | custom-call | bytes 12000000 | tf_op jit(solution)/shard_map/element_sums/pallas_call | solution.py:665
  (2 shorter events, 0.0 us)
Async XLA Ops:
  0.6 7.9 %copy-start.8 = (s32[1,128]{1,0:T(1,128)S(1)}, s32[1,128]{1,0:T(1,128)}, u32[]{:S(2)}) copy-start(s32[1,128]{1,0:T(1,128)} %counts_ref.1) | copy-start | bytes 1540
  0.6 7.9 %copy-start.7 = (f32[1,128,128]{2,1,0:T(8,128)S(1)}, f32[1,128,128]{2,1,0:T(8,128)}, u32[]{:S(2)}) copy-start(f32[1,128,128]{2,1,0:T(8,128)} %param.21) | copy-start | bytes 196612
  0.7 7.9 %copy-start.6 = (s32[1,128,128]{2,1,0:T(8,128)S(1)}, s32[1,128,128]{2,1,0:T(8,128)}, u32[]{:S(2)}) copy-start(s32[1,128,128]{2,1,0:T(8,128)} %param.20) | copy-start | bytes 196612
  0.7 7.9 %copy-start.5 = (s32[1,128,128]{2,1,0:T(8,128)S(1)}, s32[1,128,128]{2,1,0:T(8,128)}, u32[]{:S(2)}) copy-start(s32[1,128,128]{2,1,0:T(8,128)} %param.19) | copy-start | bytes 196612
  0.7 20.1 %copy-start = (s32[8,16,1024]{2,1,0:T(8,128)S(1)}, s32[8,16,1024]{2,1,0:T(8,128)}, u32[]{:S(2)}) copy-start(s32[8,16,1024]{2,1,0:T(8,128)} %solid.3) | copy-start | bytes 1572868
  3.2 13.6 %collective-permute-start.1 = (f32[5,8,1024]{2,1,0:T(8,128)}, f32[5,8,1024]{2,1,0:T(8,128)S(1)}, u32[]{:S(2)}, u32[]{:S(2)}) collective-permute-start(f32[5,8,1024]{2,1,0:T(8,128)} %get-tuple-element.72), channel_id=1, source_target_pairs={{0,1},{1,2},{2,3},{3,4},{4,5},{5,6},{6,7},{8,9},{9,10},{10,11},{11... | collective-permute-start | bytes 491528 | tf_op jit(solution)/shard_map/ppermute | solution.py:680
  7.2 9.8 %collective-permute-start = (f32[5,8,1024]{2,1,0:T(8,128)}, f32[5,8,1024]{2,1,0:T(8,128)S(1)}, u32[]{:S(2)}, u32[]{:S(2)}) collective-permute-start(f32[5,8,1024]{2,1,0:T(8,128)} %get-tuple-element.71), channel_id=1, source_target_pairs={{1,0},{2,1},{3,2},{4,3},{5,4},{6,5},{7,6},{9,8},{10,9},{11,10},{12... | collective-permute-start | bytes 491528 | tf_op jit(solution)/shard_map/ppermute | solution.py:679
  16.8 25.3 %copy-start.1 = (f32[5,8,1024]{2,1,0:T(8,128)}, f32[5,8,1024]{2,1,0:T(8,128)S(1)}, u32[]{:S(2)}) copy-start(f32[5,8,1024]{2,1,0:T(8,128)S(1)} %collective-permute-done.1.v_dn) | copy-start | bytes 491524
  17.0 25.1 %copy-start.2 = (f32[5,8,1024]{2,1,0:T(8,128)}, f32[5,8,1024]{2,1,0:T(8,128)S(1)}, u32[]{:S(2)}) copy-start(f32[5,8,1024]{2,1,0:T(8,128)S(1)} %collective-permute-done.v_up) | copy-start | bytes 491524
  17.3 24.7 %collective-permute-start.2 = (f32[5,16,1024]{2,1,0:T(8,128)S(1)}, f32[5,16,1024]{2,1,0:T(8,128)S(1)}, u32[]{:S(2)}, u32[]{:S(2)}) collective-permute-start(f32[5,16,1024]{2,1,0:T(8,128)S(1)} %scatter.15), channel_id=1, source_target_pairs={{0,120},{8,0},{16,8},{24,16},{32,24},{40,32},{48,40},{56,48},{64,5... | collective-permute-start | bytes 983048 | tf_op jit(solution)/shard_map/ppermute | solution.py:687
  18.4 23.7 %collective-permute-start.3 = (f32[5,16,1024]{2,1,0:T(8,128)S(1)}, f32[5,16,1024]{2,1,0:T(8,128)S(1)}, u32[]{:S(2)}, u32[]{:S(2)}) collective-permute-start(f32[5,16,1024]{2,1,0:T(8,128)S(1)} %scatter.19), channel_id=1, source_target_pairs={{0,8},{8,16},{16,24},{24,32},{32,40},{40,48},{48,56},{56,64},{64,7... | collective-permute-start | bytes 983048 | tf_op jit(solution)/shard_map/ppermute | solution.py:688
  42.0 20.6 %copy-start.3 = (f32[5,16,1024]{2,1,0:T(8,128)}, f32[5,16,1024]{2,1,0:T(8,128)S(1)}, u32[]{:S(2)}) copy-start(f32[5,16,1024]{2,1,0:T(8,128)S(1)} %collective-permute-done.2.h_up) | copy-start | bytes 983044
  42.0 20.6 %copy-start.4 = (f32[5,16,1024]{2,1,0:T(8,128)}, f32[5,16,1024]{2,1,0:T(8,128)S(1)}, u32[]{:S(2)}) copy-start(f32[5,16,1024]{2,1,0:T(8,128)S(1)} %collective-permute-done.3.h_dn) | copy-start | bytes 983044
  49.3 23.1 %all-to-all-start = ((f32[128,1,128]{2,1,0:T(1,128)}), f32[128,1,128]{2,1,0:T(1,128)S(1)}, u32[]{:S(2)}, u32[]{:S(2)}) async-start(f32[128,1,128]{2,1,0:T(1,128)} %bitcast.8), calls=%async_computation | async-start | bytes 131072 | tf_op jit(solution)/shard_map/all_to_all | solution.py:692
  72.4 0.6 copy-start.9

commit v3 on v2

--- a/solution.py
+++ b/solution.py
@@ -48,6 +48,7 @@
 SMEM = pl.BlockSpec(memory_space=pltpu.SMEM)
 HBM = pl.BlockSpec(memory_space=pltpu.HBM)
 SPAN_PAIRS = [p for p in range(PAIRS) if VECS[2 * p + 1][0] != 0]
+VERT_PAIRS = [p for p in range(PAIRS) if VECS[2 * p + 1][1] != 0]
 SIDE_ROWS = 5 * CV * COLS
 RIM_ROWS = 2 * SIDE_ROWS + 2 * 5 * CS * COLS
 GROUPS = CAP // 8
@@ -181,6 +182,21 @@
     return compacted(flag, place, place, ahead, behind, LISTED)
 
 
+def row_lists(flag, value, rows, pos, listed):
+    lane = lax.broadcasted_iota(jnp.int32, (OWNERS, CAP), 1)
+    front, count = compacted(
+        flag, value, lane,
+        lambda x, d: pltpu.roll(x, CAP - d, 1), lambda x, d: pltpu.roll(x, d, 1), CAP,
+    )
+    rows[...] = front
+    pos[...] = jnp.where(flag == 1, count - 1, -1)
+    totals = jnp.transpose(count.astype(jnp.float32))[CAP - 1 : CAP, :].astype(jnp.int32)
+    ids, running = group_list((totals + 7) >> 3)
+    listed[0:GROUPS, :] = ids
+    listed[GROUPS : 2 * GROUPS, :] = running
+    listed[2 * GROUPS : 2 * GROUPS + 8, :] = jnp.broadcast_to(jnp.max(totals, axis=1, keepdims=True), (8, LANES))
+
+
 def faces_kernel(adj, hv_up, hv_dn, tiles, sem):
     copies = []
     for k, i in enumerate(VERT_UP):
@@ -198,7 +214,7 @@
                 hv_dn[k - 5, s : s + 1, :] = tiles[k, s, 7:8, :]
 
 
-CHUNKS = 4
+CHUNKS = 2
 STEP = CS // CHUNKS
 N_LOAD = 13
 
@@ -221,8 +237,8 @@
 
 def tables_kernel(
     cells_ref, dirs_ref, weight_ref, counts_ref, adj,
-    table, hs_up, hs_dn, ridx, hidx, lidx, pos, weight, list_a, list_b,
-    wide, tilted, load_sem, face_sem,
+    table, hs_up, hs_dn, ridx, lidx, pos, weight, list_a, rim_code,
+    wide, tbuf, tilted, load_sem, face_sem, out_sem,
 ):
     copies = [load_copies(adj, wide, load_sem, q, STEP * q, STEP * (q + 1), 0) for q in range(CHUNKS)]
     faces = []
@@ -249,7 +265,6 @@
     v = (cells >> 10) & 15
     s = cells >> 14
     in_slab = (v >> 3) * 64 + xc * 8 + (v & 7)
-    ridx[...] = pair * 1024 + s * 128 + in_slab
     lidx[...] = cells & 127
     lane = lax.broadcasted_iota(jnp.int32, (OWNERS, CAP), 1)
     counts = jnp.broadcast_to(counts_ref[...].astype(jnp.float32), (OWNERS, OWNERS))
@@ -264,21 +279,10 @@
     on_v = has_v & ((v == 0) | (v == CV - 1))
     at_s = (jnp.where(s == 0, 0, 5) + k_s) * 128 + in_slab
     at_v = 2 * SIDE_ROWS + ((jnp.where(v == 0, 0, 5) + k_v) * 8 + xc) * 8 + s
-    flag = jnp.where(live & (on_s | on_v), 1, 0)
-    where_rim = jnp.where(on_s, at_s, at_v)
-    rows, count = compacted(
-        flag, where_rim, lane,
-        lambda x, d: pltpu.roll(x, CAP - d, 1), lambda x, d: pltpu.roll(x, d, 1), CAP,
-    )
-    hidx[...] = rows
-    pos[...] = jnp.where(flag == 1, count - 1, -1)
-    totals = jnp.transpose(count.astype(jnp.float32))[CAP - 1 : CAP, :].astype(jnp.int32)
-    for out, groups in ((list_a, (counts_ref[...] + 7) >> 3), (list_b, (totals + 7) >> 3)):
-        ids, running = group_list(groups)
-        out[0:GROUPS, :] = ids
-        out[GROUPS : 2 * GROUPS, :] = running
-    list_b[2 * GROUPS : 2 * GROUPS + 8, :] = jnp.broadcast_to(jnp.max(totals, axis=1, keepdims=True), (8, LANES))
-    list_a[2 * GROUPS : 2 * GROUPS + 8, :] = jnp.zeros((8, LANES), jnp.int32)
+    on_rim = on_s | on_v
+    rim_code[...] = jnp.where(live & on_rim, jnp.where(on_s, at_s, at_v), -1)
+    flag = jnp.where(live & jnp.logical_not(on_rim), 1, 0)
+    row_lists(flag, pair * 1024 + s * 128 + in_slab, ridx, pos, list_a)
 
     def slab(s, carry):
         def column(i, xt):
@@ -289,8 +293,10 @@
             for p in range(PAIRS):
                 diff = pulled(2 * p + 1, xt) - pulled(2 * p + 2, xt)
                 for vt in range(2):
-                    at = pl.multiple_of(s * 128 + (p * 1024 + 64 * vt + 8 * xt), 8)
-                    table[pl.ds(at, 8), :] = diff[8 * vt : 8 * vt + 8]
+                    at = pl.multiple_of(s * 128 + (64 * vt + 8 * xt), 8)
+                    tbuf[p, pl.ds(at, 8), :] = diff[8 * vt : 8 * vt + 8]
+        rows = pl.ds(pl.multiple_of(s * 128, 128), 128)
+        pltpu.make_async_copy(tbuf.at[:, rows], table.at[:, rows], out_sem.at[s]).start()
         return carry
 
     for q in range(CHUNKS):
@@ -302,6 +308,9 @@
     for n, cv, out, k in tilts:
         for xt in range(COLS):
             out[k, :, col(xt)] = vert_shifted(tilted[n, :, col(xt)], None, cv)
+    for s in range(CS):
+        rows = pl.ds(s * 128, 128)
+        pltpu.make_async_copy(tbuf.at[:, rows], table.at[:, rows], out_sem.at[s]).wait()
 
 
 PER_TURN = 32
@@ -318,6 +327,15 @@
     picked[group] = jnp.take_along_axis(v, lrow, axis=1)
 
 
+def placed(t, groups, pos, picked):
+    sub = lax.broadcasted_iota(jnp.int32, (8, LANES), 0)
+    posb = jnp.broadcast_to(pos[pl.ds(t, 1), :], (8, LANES))
+    acc = jnp.zeros((8, LANES), jnp.float32)
+    for g in groups:
+        acc = jnp.where(posb == sub + 8 * g, picked[t * GROUPS + g], acc)
+    return jnp.sum(acc, axis=0, keepdims=True)
+
+
 def pick_rest(start, listed, index, table, lidx, picked):
     total = listed[2 * LISTED - 1]
 
@@ -352,15 +370,30 @@
     )
 
 
-BESIDE = 24
+BESIDE = 27
+
+
+def scalar_copies(index_ref, listed_ref, index, listed, sem):
+    copies = [
+        pltpu.make_async_copy(index_ref, index, sem.at[0]),
+        pltpu.make_async_copy(listed_ref, listed, sem.at[1]),
+    ]
+    for c in copies:
+        c.start()
+    return copies
+
+
 IN_CHUNKS = 3
 IN_STEP = INNER // IN_CHUNKS
 
 
 def inner_kernel(
-    index, listed, lidx, table, v_up, v_dn, adj, saved, solid,
-    out, local, picked, wide, sav, sol, obuf, vup, vdn, load_sem, misc_sem, out_sem,
+    index_ref, listed_ref, lidx, pos, rim_code, v_up, v_dn, table_ref, adj, saved, solid,
+    out, local, rim_index, rim_pos, rim_listed, near, index, listed, scalar_sem, table, table_sem, picked, wide, sav, sol, obuf, vup, vdn, load_sem, misc_sem, out_sem,
 ):
+    scalars = scalar_copies(index_ref, listed_ref, index, listed, scalar_sem)
+    scalars.append(pltpu.make_async_copy(table_ref, table, table_sem.at[0]))
+    scalars[-1].start()
     copies = []
     for q in range(IN_CHUNKS):
         lo = 1 + IN_STEP * q
@@ -371,6 +404,8 @@
         for c in copies[q]:
             c.start()
     fill_rims(v_up, v_dn, vup, vdn)
+    code = rim_code[...]
+    row_lists(jnp.where(code >= 0, 1, 0), jnp.maximum(code, 0), rim_index, rim_pos, rim_listed)
 
     def slab(n, carry):
         def column(i, xt):
@@ -389,25 +424,31 @@
         pltpu.make_async_copy(obuf.at[:, n], out.at[:, n + 1], out_sem.at[n]).start()
         return carry
 
+    for c in scalars:
+        c.wait()
     for q in range(IN_CHUNKS):
         for c in copies[q]:
             c.wait()
         lax.fori_loop(IN_STEP * q, IN_STEP * (q + 1), slab, 0)
     pick_rest(INNER * COLS * BESIDE, listed, index, table, lidx, picked)
-    sub = lax.broadcasted_iota(jnp.int32, (8, LANES), 0)
-    lane = lax.broadcasted_iota(jnp.int32, (8, LANES), 1)
 
     def turn(b, carry):
-        for q in range(8):
-            t = b * 8 + q
-            acc = picked[t * GROUPS]
-            for g in range(1, GROUPS):
-                acc = jnp.where((lane >> 3) == g, picked[t * GROUPS + g], acc)
-            acc = jnp.where((lane & 7) == sub, acc, 0.0)
-            local[pl.ds(t, 1), :] = jnp.sum(acc, axis=0, keepdims=True)
+        for q in range(16):
+            t = b * 16 + q
+            local[pl.ds(t, 1), :] = placed(t, range(GROUPS), pos, picked)
         return carry
 
-    lax.fori_loop(0, OWNERS // 8, turn, 0)
+    lax.fori_loop(0, OWNERS // 16, turn, 0)
+    for side, s in ((0, 0), (1, CS - 1)):
+        for k, p in enumerate(SPAN_PAIRS):
+            at = (side * 5 + k) * 128
+            own = p * 1024 + s * 128
+            near[at : at + 128, :] = table[own : own + 128, :]
+        for k, p in enumerate(VERT_PAIRS):
+            for xt in range(COLS):
+                at = 2 * SIDE_ROWS + ((side * 5 + k) * 8 + xt) * 8
+                own = p * 1024 + (71 if side == 1 else 0) + 8 * xt
+                near[at : at + 8, :] = table[pl.ds(own, CS, stride=128), :]
     for n in range(INNER):
         pltpu.make_async_copy(obuf.at[:, n], out.at[:, n + 1], out_sem.at[n]).wait()
 
@@ -416,8 +457,10 @@
 
 
 def rim_kernel(
-    index, listed, lidx, pos, weight, local, h_up, h_dn, v_up, v_dn, values, rim, picked,
+    index_ref, listed_ref, lidx, pos, weight, local, near, h_up, h_dn, v_up, v_dn, values,
+    index, listed, scalar_sem, rim, picked,
 ):
+    scalars = scalar_copies(index_ref, listed_ref, index, listed, scalar_sem)
     for side, s, halo, pops in ((0, 0, h_dn, SPAN_DOWN), (1, CS - 1, h_up, SPAN_UP)):
         def column(i, xt):
             cs, cv, _ = VECS[i]
@@ -436,9 +479,8 @@
                     d = pulled(plus, xt) if plus in pops else -pulled(minus, xt)
                 for vt in range(2):
                     at = (side * 5 + k) * 128 + 64 * vt + 8 * xt
-                    rim[at : at + 8, :] = d[8 * vt : 8 * vt + 8]
+                    rim[at : at + 8, :] = d[8 * vt : 8 * vt + 8] + near[at : at + 8, :]
     lane = lax.broadcasted_iota(jnp.int32, (8, LANES), 1)
-    sub = lax.broadcasted_iota(jnp.int32, (8, LANES), 0)
     for side, halo, pops in ((0, v_dn, VERT_DOWN), (1, v_up, VERT_UP)):
         for k, i in enumerate(pops):
             cs, _, cx = VECS[i]
@@ -451,33 +493,29 @@
                 cols = [jnp.where(lane == edge, rolled[(xt + cx) % COLS], rolled[xt]) for xt in range(COLS)]
             for xt in range(COLS):
                 at = 2 * SIDE_ROWS + ((side * 5 + k) * 8 + xt) * 8
-                rim[at : at + 8, :] = cols[xt] if i % 2 == 1 else -cols[xt]
-
+                here = near[at : at + 8, :]
+                rim[at : at + 8, :] = here + cols[xt] if i % 2 == 1 else here - cols[xt]
+
+    for c in scalars:
+        c.wait()
     pick_rest(0, listed, index, rim, lidx, picked)
     most = listed[2 * LISTED]
 
-    def added(t, groups):
-        posb = jnp.broadcast_to(pos[pl.ds(t, 1), :], (8, LANES))
-        acc = jnp.zeros((8, LANES), jnp.float32)
-        for g in groups:
-            acc = acc + jnp.where(posb == sub + 8 * g, picked[t * GROUPS + g], 0.0)
-        return jnp.sum(acc, axis=0, keepdims=True)
-
     def turn(b, carry):
-        for q in range(8):
-            t = b * 8 + q
+        for q in range(16):
+            t = b * 16 + q
             w = weight[pl.ds(t, 1), :]
-            total = local[pl.ds(t, 1), :] + added(t, range(FIRST))
+            total = local[pl.ds(t, 1), :] + placed(t, range(FIRST), pos, picked)
             values[pl.ds(t, 1), :] = jnp.where(w == 0.0, 0.0, w * total)
         return carry
 
-    lax.fori_loop(0, OWNERS // 8, turn, 0)
+    lax.fori_loop(0, OWNERS // 16, turn, 0)
 
     @pl.when(most > 8 * FIRST)
     def _():
         def more(t, carry):
             w = weight[pl.ds(t, 1), :]
-            rest = w * added(t, range(FIRST, GROUPS))
+            rest = w * placed(t, range(FIRST, GROUPS), pos, picked)
             values[pl.ds(t, 1), :] = values[pl.ds(t, 1), :] + jnp.where(w == 0.0, 0.0, rest)
             return carry
 
@@ -485,9 +523,11 @@
 
 
 def outer_kernel(
-    h_up, h_dn, v_up, v_dn, adj, saved, solid, partial, out, wide, sav, sol, obuf, load_sem, out_sem,
+    h_up, h_dn, v_up, v_dn, adj, saved, solid, recv, partial, out, slots, wide, sav, sol, obuf, load_sem, out_sem, slot_sem,
 ):
     del partial
+    fetch = pltpu.make_async_copy(recv, slots, slot_sem.at[0])
+    fetch.start()
     ends = ((0, 0, h_dn, SPAN_DOWN), (1, CS - 1, h_up, SPAN_UP))
     copies = []
     for n, s, halo, pops in ends:
@@ -522,6 +562,7 @@
         pltpu.make_async_copy(obuf.at[:, n], out.at[:, s], out_sem.at[n]).start()
     for n, s, halo, pops in ends:
         pltpu.make_async_copy(obuf.at[:, n], out.at[:, s], out_sem.at[n]).wait()
+    fetch.wait()
 
 
 def sums_kernel(slots, received, out):
@@ -529,25 +570,19 @@
     sub_lo = lax.broadcasted_iota(jnp.int32, (LANES, 2 * LANES), 0)
     sub_hi = lax.broadcasted_iota(jnp.int32, (his, 2 * LANES), 0)
 
-    def turn(t, acc):
-        for q in range(8):
-            r = (t * 8 + q) * 2
-            slot = jnp.concatenate([slots[pl.ds(r, 1), :], slots[pl.ds(r + 1, 1), :]], 1)
-            v0 = jnp.concatenate([received[r], received[r + 1]], 1)
-            a = v0.astype(jnp.bfloat16).astype(jnp.float32)
-            b = (v0 - a).astype(jnp.bfloat16).astype(jnp.float32)
-            c = (v0 - a) - b
-            hit = jnp.broadcast_to(slot >> 7, (his, 2 * LANES)) == sub_hi
-            left = jnp.concatenate(
-                [jnp.where(hit, jnp.broadcast_to(v, (his, 2 * LANES)), 0.0).astype(jnp.bfloat16) for v in (a, b, c)], 0
-            )
-            right = jnp.where(jnp.broadcast_to(slot & 127, (LANES, 2 * LANES)) == sub_lo, 1.0, 0.0).astype(jnp.bfloat16)
-            acc = acc + lax.dot_general(
-                left, right, (((1,), (1,)), ((), ())), preferred_element_type=jnp.float32
-            )
-        return acc
-
-    acc = lax.fori_loop(0, OWNERS // 16, turn, jnp.zeros((3 * his, LANES), jnp.float32))
+    acc = jnp.zeros((3 * his, LANES), jnp.float32)
+    for r in range(0, OWNERS, 2):
+        slot = jnp.concatenate([slots[r : r + 1, :], slots[r + 1 : r + 2, :]], 1)
+        v0 = jnp.concatenate([received[r], received[r + 1]], 1)
+        a = v0.astype(jnp.bfloat16).astype(jnp.float32)
+        b = (v0 - a).astype(jnp.bfloat16).astype(jnp.float32)
+        c = (v0 - a) - b
+        hit = jnp.broadcast_to(slot >> 7, (his, 2 * LANES)) == sub_hi
+        left = jnp.concatenate(
+            [jnp.where(hit, jnp.broadcast_to(v, (his, 2 * LANES)), 0.0).astype(jnp.bfloat16) for v in (a, b, c)], 0
+        )
+        right = jnp.where(jnp.broadcast_to(slot & 127, (LANES, 2 * LANES)) == sub_lo, 1.0, 0.0).astype(jnp.bfloat16)
+        acc = acc + lax.dot_general(left, right, (((1,), (1,)), ((), ())), preferred_element_type=jnp.float32)
     out[...] = acc[0:his] + acc[his : 2 * his] + acc[2 * his : 3 * his]
 
 
@@ -585,17 +620,19 @@
     return pl.pallas_call(
         tables_kernel,
         out_shape=(
-            shape((ROWS, LANES)), shape((5, CV, NX)), shape((5, CV, NX)),
-            shape(GRID, I32), shape(GRID, I32), shape(GRID, I32), shape(GRID, I32), shape(GRID),
-            shape((40, LANES), I32), shape((40, LANES), I32),
+            shape((PAIRS, ROWS // PAIRS, LANES)), shape((5, CV, NX)), shape((5, CV, NX)),
+            shape(GRID, I32), shape(GRID, I32), shape(GRID, I32), shape(GRID),
+            shape((40, LANES), I32), shape(GRID, I32),
         ),
         in_specs=[VMEM] * 4 + [HBM],
-        out_specs=(VMEM,) * 10,
+        out_specs=(HBM,) + (VMEM,) * 8,
         scratch_shapes=[
             pltpu.VMEM((Q, CS, CV, NX), F32),
+            pltpu.VMEM((PAIRS, ROWS // PAIRS, LANES), F32),
             pltpu.VMEM((4, CV, NX), F32),
             pltpu.SemaphoreType.DMA((CHUNKS, N_LOAD)),
             pltpu.SemaphoreType.DMA((10,)),
+            pltpu.SemaphoreType.DMA((CS,)),
         ],
         compiler_params=limit(50),
         cost_estimate=cost(8),
@@ -603,13 +640,21 @@
     )(cells, dirs, weight, counts, adjoint)
 
 
-def inner_call(ridx, list_a, lidx, table, v_up, v_dn, adjoint, saved, solid):
+SCALARS = [pltpu.SMEM((OWNERS * CAP,), I32), pltpu.SMEM((40 * LANES,), I32), pltpu.SemaphoreType.DMA((2,))]
+
+
+def inner_call(ridx, list_a, lidx, pos, rim_code, table, v_up, v_dn, adjoint, saved, solid):
     return pl.pallas_call(
         inner_kernel,
-        out_shape=(shape((Q, CS, CV, NX)), shape(GRID)),
-        in_specs=[SMEM, SMEM] + [VMEM] * 4 + [HBM] * 3,
-        out_specs=(HBM, VMEM),
-        scratch_shapes=[
+        out_shape=(
+            shape((Q, CS, CV, NX)), shape(GRID), shape(GRID, I32), shape(GRID, I32), shape((40, LANES), I32),
+            shape((RIM_ROWS, LANES)),
+        ),
+        in_specs=[VMEM] * 7 + [HBM] * 4,
+        out_specs=(HBM,) + (VMEM,) * 5,
+        scratch_shapes=SCALARS + [
+            pltpu.VMEM((ROWS, LANES), F32),
+            pltpu.SemaphoreType.DMA((1,)),
             pltpu.VMEM((LISTED, 8, LANES), F32),
             pltpu.VMEM((Q, INNER, CV, NX), F32),
             pltpu.VMEM((Q, INNER, CV, NX), jnp.bfloat16),
@@ -624,28 +669,31 @@
         compiler_params=limit(50),
         cost_estimate=cost(15),
         name="inner",
-    )(ridx.reshape(-1), list_a.reshape(-1), lidx, table, v_up, v_dn, adjoint, saved, solid)
-
-
-def rim_call(hidx, list_b, lidx, pos, weight, local, h_up, h_dn, v_up, v_dn):
+    )(ridx.reshape(-1), list_a.reshape(-1), lidx, pos, rim_code, v_up, v_dn, table.reshape(ROWS, LANES), adjoint, saved, solid)
+
+
+def rim_call(hidx, list_b, lidx, pos, weight, local, near, h_up, h_dn, v_up, v_dn):
     return pl.pallas_call(
         rim_kernel,
         out_shape=shape(GRID),
-        in_specs=[SMEM, SMEM] + [VMEM] * 8,
+        in_specs=[VMEM] * 11,
         out_specs=VMEM,
-        scratch_shapes=[pltpu.VMEM((RIM_ROWS, LANES), F32), pltpu.VMEM((LISTED, 8, LANES), F32)],
+        scratch_shapes=SCALARS + [pltpu.VMEM((RIM_ROWS, LANES), F32), pltpu.VMEM((LISTED, 8, LANES), F32)],
         compiler_params=limit(50),
         cost_estimate=cost(5),
         name="rim",
-    )(hidx.reshape(-1), list_b.reshape(-1), lidx, pos, weight, local, h_up, h_dn, v_up, v_dn)
-
-
-def outer_call(h_up, h_dn, v_up, v_dn, adjoint, saved, solid, partial):
+    )(hidx.reshape(-1), list_b.reshape(-1), lidx, pos, weight, local, near, h_up, h_dn, v_up, v_dn)
+
+
+OUTER_MIB = 53
+
+
+def outer_call(h_up, h_dn, v_up, v_dn, adjoint, saved, solid, recv, partial):
     return pl.pallas_call(
         outer_kernel,
-        out_shape=shape((Q, CS, CV, NX)),
-        in_specs=[VMEM] * 4 + [HBM] * 4,
-        out_specs=HBM,
+        out_shape=(shape((Q, CS, CV, NX)), shape(GRID, I32)),
+        in_specs=[VMEM] * 4 + [HBM] * 5,
+        out_specs=(HBM, VMEM),
         scratch_shapes=[
             pltpu.VMEM((Q, 2, CV, NX), F32),
             pltpu.VMEM((Q, 2, CV, NX), jnp.bfloat16),
@@ -653,12 +701,13 @@
             pltpu.VMEM((Q, 2, CV, NX), F32),
             pltpu.SemaphoreType.DMA((2, 10)),
             pltpu.SemaphoreType.DMA((2,)),
+            pltpu.SemaphoreType.DMA((1,)),
         ],
-        input_output_aliases={7: 0},
-        compiler_params=limit(56),
+        input_output_aliases={8: 0},
+        compiler_params=limit(OUTER_MIB),
         cost_estimate=cost(3),
         name="outer",
-    )(h_up, h_dn, v_up, v_dn, adjoint, saved, solid, partial)
+    )(h_up, h_dn, v_up, v_dn, adjoint, saved, solid, recv, partial)
 
 
 def sums_call(slots, received):
@@ -667,6 +716,7 @@
         out_shape=shape((ELEM_DEV // LANES, LANES)),
         in_specs=[VMEM, VMEM],
         out_specs=VMEM,
+        compiler_params=limit(16),
         cost_estimate=cost(4),
         name="element_sums",
     )(slots, received)
@@ -678,7 +728,7 @@
     hv_up, hv_dn = faces_call(adjoint)
     v_up = lax.ppermute(hv_up, "vert", [(i, i - 1) for i in range(1, nv)])
     v_dn = lax.ppermute(hv_dn, "vert", [(i, i + 1) for i in range(nv - 1)])
-    table, hs_up, hs_dn, ridx, hidx, lidx, pos, weight, list_a, list_b = tables_call(
+    table, hs_up, hs_dn, ridx, lidx, pos, weight, list_a, rim_code = tables_call(
         send_cells[0], send_dirs[0], send_weight[0], send_counts, adjoint
     )
     hs_up = hs_up.at[1, CV - 1].set(v_up[1, 0]).at[2, 0].set(v_dn[2, 0])
@@ -686,12 +736,14 @@
     hs_up, hs_dn, list_a = lax.optimization_barrier((hs_up, hs_dn, list_a))
     h_up = lax.ppermute(hs_up, "span", [(i, (i - 1) % ns) for i in range(ns)])
     h_dn = lax.ppermute(hs_dn, "span", [(i, (i + 1) % ns) for i in range(ns)])
-    partial, local = inner_call(ridx, list_a, lidx, table, v_up, v_dn, adjoint, saved, solid)
-    values = rim_call(hidx, list_b, lidx, pos, weight, local, h_up, h_dn, v_up, v_dn)
+    partial, local, rim_index, rim_pos, list_b, near = inner_call(
+        ridx, list_a, lidx, pos, rim_code, table, v_up, v_dn, adjoint, saved, solid
+    )
+    values = rim_call(rim_index, list_b, lidx, rim_pos, weight, local, near, h_up, h_dn, v_up, v_dn)
     values, v_up, v_dn = lax.optimization_barrier((values, v_up, v_dn))
     received = lax.all_to_all(values[:, None, :], ("span", "vert"), split_axis=0, concat_axis=0, tiled=True)
-    adjoint_prev = outer_call(h_up, h_dn, v_up, v_dn, adjoint, saved, solid, partial)
-    sens = sums_call(recv_slots[0], received)
+    adjoint_prev, slots = outer_call(h_up, h_dn, v_up, v_dn, adjoint, saved, solid, recv_slots[0], partial)
+    sens = sums_call(slots, received)
     return adjoint_prev, sens.reshape(ELEM_DEV)
 
 

time: 77.3 us -> 69.8 us (0.903)
  Pallas kernels: 48.3 us -> 39.3 us
  starting transfers between devices: 22 us -> 24.5 us
    pallas_call x1, Pallas kernels: 21.2 us -> 16.8 us  [inner_call(): pl.pallas_call(inner_kernel, out_shape=(shape((Q, CS, CV, NX)), shape(GRI...]
    pallas_call x3, Pallas kernels: 20.6 us -> 17.9 us  [the longest x1 7.59 us: tables_call(): pl.pallas_call(tables_kernel, out_shape=(shape((PAIRS, ROWS // PAIRS, LAN...]
    all_to_all x1, starting transfers between devices: 13.4 us -> 15.4 us  [body(): lax.all_to_all(values[:, None, :], ('span', 'vert'), split_axis=0, concat...]
    pallas_call x1, Pallas kernels: 3.98 us -> 2.06 us  [sums_call(): pl.pallas_call(sums_kernel, out_shape=shape((ELEM_DEV // LANES, LANES)),...]
  transfers between devices with their start and end apart: 5 -> 5, of which waited for: 1 -> 1; matrix products, arithmetic and copies ran while one was open for 0% -> 0% of each run, Pallas kernels for 45% -> 42%
where the time goes in v3:
time: 69.8 us
  Pallas kernels  39.3 us (56%)
  starting transfers between devices  24.5 us (35%)
  waiting for transfers between devices  4.69 us (7%)
  between operations  0.87 us (1%)
    pallas_call x1, Pallas kernels, inner_call(): pl.pallas_call(inner_kernel, out_shape=(shape((Q, CS, CV, NX)), shape(GRI...  16.8 us
    all_to_all x1, starting transfers between devices, body(): lax.all_to_all(values[:, None, :], ('span', 'vert'), split_axis=0, concat...  15.4 us
    pallas_call x1, Pallas kernels, tables_call(): pl.pallas_call(tables_kernel, out_shape=(shape((PAIRS, ROWS // PAIRS, LAN...  7.59 us
    pallas_call x1, Pallas kernels, rim_call(): pl.pallas_call(rim_kernel, out_shape=shape(GRID), in_specs=[VMEM] * 11, o...  5.3 us
    pallas_call x1, Pallas kernels, outer_call(): pl.pallas_call(outer_kernel, out_shape=(shape((Q, CS, CV, NX)), shape(GRI...  4.99 us
    all_to_all x1, waiting for transfers between devices, body(): lax.all_to_all(values[:, None, :], ('span', 'vert'), split_axis=0, concat...  4.68 us
    ppermute x1, starting transfers between devices, body(): v_dn = lax.ppermute(hv_dn, 'vert', [(i, i + 1) for i in range(nv - 1)])  3.95 us
    ppermute x1, starting transfers between devices, body(): h_dn = lax.ppermute(hs_dn, 'span', [(i, (i + 1) % ns) for i in range(ns)])  2.71 us
  transfers between devices with their start and end apart: 5, of which 1 were waited for; matrix products, arithmetic and copies ran while one was open for 0% of the time, Pallas kernels for 42%

profile of v3, /device:TPU:1, one launch (start us, length us, event | category | flops | bytes accessed | tf_op | source)
XLA Modules:
  0.0 69.8 jit_solution(5280763070731650418)
XLA Ops:
  0.6 0.0 copy-start.6
  0.6 0.0 copy-start.4
  0.7 0.0 copy-start.3
  0.7 0.0 copy-start.2
  0.7 0.0 copy-start
  0.7 2.5 %faces.1 = (f32[5,8,1024]{2,1,0:T(8,128)}, f32[5,8,1024]{2,1,0:T(8,128)}) custom-call(f32[19,8,16,1024]{3,2,1,0:T(8,128)} %adj.7), custom_call_target="tpu_custom_call" | custom-call | bytes 6000000 | tf_op jit(solution)/shard_map/faces/pallas_call | solution.py:607
  3.2 4.0 %collective-permute-start.1 = (f32[5,8,1024]{2,1,0:T(8,128)}, f32[5,8,1024]{2,1,0:T(8,128)S(1)}, u32[]{:S(2)}, u32[]{:S(2)}) collective-permute-start(f32[5,8,1024]{2,1,0:T(8,128)} %get-tuple-element.77), channel_id=1, source_target_pairs={{0,1},{1,2},{2,3},{3,4},{4,5},{5,6},{6,7},{8,9},{9,10},{10,11},{11... | collective-permute-start | bytes 491528 | tf_op jit(solution)/shard_map/ppermute | solution.py:730
  7.2 1.3 %collective-permute-start = (f32[5,8,1024]{2,1,0:T(8,128)}, f32[5,8,1024]{2,1,0:T(8,128)S(1)}, u32[]{:S(2)}, u32[]{:S(2)}) collective-permute-start(f32[5,8,1024]{2,1,0:T(8,128)} %get-tuple-element.76), channel_id=1, source_target_pairs={{1,0},{2,1},{3,2},{4,3},{5,4},{6,5},{7,6},{9,8},{10,9},{11,10},{12... | collective-permute-start | bytes 491528 | tf_op jit(solution)/shard_map/ppermute | solution.py:729
  8.5 0.0 copy-done.6
  8.5 0.0 copy-done.4
  8.5 0.0 copy-done.3
  8.5 0.0 copy-done.2
  8.5 7.6 %tables.1 = (f32[9,1024,128]{2,1,0:T(8,128)}, f32[5,16,1024]{2,1,0:T(8,128)S(1)}, f32[5,16,1024]{2,1,0:T(8,128)S(1)}, s32[128,128]{1,0:T(8,128)S(1)}, s32[128,12...) custom-call(s32[128,128]{1,0:T(8,128)S(1)} %bitcast.11, ...), custom_call_target="tpu_custom_call" | custom-call | bytes 24000000 | tf_op jit(solution)/shard_map/tables/pallas_call | solution.py:620
  16.1 0.0 collective-permute-done.1.v_dn
  16.2 0.1 scatter.16
  16.3 0.0 collective-permute-done.v_up
  16.3 0.1 scatter.14
  16.4 0.1 scatter.19
  16.5 0.1 scatter.15
  16.7 1.1 %collective-permute-start.2 = (f32[5,16,1024]{2,1,0:T(8,128)S(1)}, f32[5,16,1024]{2,1,0:T(8,128)S(1)}, u32[]{:S(2)}, u32[]{:S(2)}) collective-permute-start(f32[5,16,1024]{2,1,0:T(8,128)S(1)} %scatter.15), channel_id=1, source_target_pairs={{0,120},{8,0},{16,8},{24,16},{32,24},{40,32},{48,40},{56,48},{64,5... | collective-permute-start | bytes 983048 | tf_op jit(solution)/shard_map/ppermute | solution.py:737
  17.7 2.7 %collective-permute-start.3 = (f32[5,16,1024]{2,1,0:T(8,128)S(1)}, f32[5,16,1024]{2,1,0:T(8,128)S(1)}, u32[]{:S(2)}, u32[]{:S(2)}) collective-permute-start(f32[5,16,1024]{2,1,0:T(8,128)S(1)} %scatter.19), channel_id=1, source_target_pairs={{0,8},{8,16},{16,24},{24,32},{32,40},{40,48},{48,56},{56,64},{64,7... | collective-permute-start | bytes 983048 | tf_op jit(solution)/shard_map/ppermute | solution.py:738
  20.4 0.0 copy-done
  20.5 0.0 copy-start.5
  20.5 16.8 %inner.1 = (f32[19,8,16,1024]{3,2,1,0:T(8,128)}, f32[128,128]{1,0:T(8,128)S(1)}, s32[128,128]{1,0:T(8,128)S(1)}, s32[128,128]{1,0:T(8,128)S(1)}, s32[40,128]{1,0:T(8,128)S(1)}, /*index=5*/f32[1920,128]{1,0:T(8,128)S(1)}) custom-call(s32[16384]{0:T(1024)S(1)} %bitcast.15, s32[5120]{0:T(1024)S(1)} %bitcast.17, s32[128,128]{1,0:T(8,128)S(1)} %get-tuple-element.84.lidx, ...), custom_call_target="tpu_custom_call" | custom-call | bytes 45000000 | tf_op jit(solution)/shard_map/inner/pallas_call | solution.py:647
  37.3 0.0 collective-permute-done.2.h_up
  37.3 0.0 collective-permute-done.3.h_dn
  37.3 0.0 copy-start.1
  37.3 5.3 %rim.1 = f32[128,128]{1,0:T(8,128)} custom-call(s32[16384]{0:T(1024)S(1)} %bitcast.16, s32[5120]{0:T(1024)S(1)} %bitcast.18, s32[128,128]{1,0:T(8,128)S(1)} %get-tuple-element.84.lidx, s32[128,128]{1,0:T(8,128)S(1)} %get-tuple-element.90.pos, f32[128,128]{1,0:T(8,128)S(1)} %get-tuple-element.91.weight, f32[128,128]{1,0:T(8,128)S(1)} %get-tuple-element.92.local, ...), custom_call_target="tpu_custom_call" | custom-call | bytes 15000000 | tf_op jit(solution)/shard_map/rim/pallas_call | solution.py:676
  42.6 15.4 %all-to-all-start = ((f32[128,1,128]{2,1,0:T(1,128)}), f32[128,1,128]{2,1,0:T(1,128)S(1)}, u32[]{:S(2)}, u32[]{:S(2)}) async-start(f32[128,1,128]{2,1,0:T(1,128)} %bitcast.9), calls=%async_computation | async-start | bytes 131072 | tf_op jit(solution)/shard_map/all_to_all | solution.py:744
  58.0 0.0 copy-done.1
  58.1 0.0 copy-done.5
  58.1 5.0 %outer.1 = (f32[19,8,16,1024]{3,2,1,0:T(8,128)}, s32[128,128]{1,0:T(8,128)S(1)}) custom-call(f32[5,16,1024]{2,1,0:T(8,128)S(1)} %collective-permute-done.2.h_up, f32[5,16,1024]{2,1,0:T(8,128)} %copy-done.1, f32[5,8,1024]{2,1,0:T(8,128)S(1)} %collective-permute-done.v_up, ...), custom_call_target="tpu_custom_call", output_to_operand_aliasing={{0}: (8, {})} | custom-call | bytes 9000000 | tf_op jit(solution)/shard_map/outer/pallas_call | solution.py:692
  63.1 4.7 %all-to-all-done.received = f32[128,1,128]{2,1,0:T(1,128)S(1)} async-done(((f32[128,1,128]{2,1,0:T(1,128)}), f32[128,1,128]{2,1,0:T(1,128)S(1)}, u32[]{:S(2)}, u32[]{:S(2)}) %all-to-all-start) | async-done | bytes 65568 | tf_op jit(solution)/shard_map/all_to_all | solution.py:744
  67.7 2.1 %element_sums.1 = f32[32,128]{1,0:T(8,128)} custom-call(s32[128,128]{1,0:T(8,128)S(1)} %get-tuple-element.98.slots, f32[128,1,128]{2,1,0:T(1,128)S(1)} %all-to-all-done.received), custom_call_target="tpu_custom_call" | custom-call | bytes 12000000 | tf_op jit(solution)/shard_map/element_sums/pallas_call | solution.py:714
  (2 shorter events, 0.0 us)
Async XLA Ops:
  0.6 7.9 %copy-start.6 = (s32[1,128]{1,0:T(1,128)S(1)}, s32[1,128]{1,0:T(1,128)}, u32[]{:S(2)}) copy-start(s32[1,128]{1,0:T(1,128)} %counts_ref.1) | copy-start | bytes 1540
  0.6 7.9 %copy-start.4 = (f32[1,128,128]{2,1,0:T(8,128)S(1)}, f32[1,128,128]{2,1,0:T(8,128)}, u32[]{:S(2)}) copy-start(f32[1,128,128]{2,1,0:T(8,128)} %param.21) | copy-start | bytes 196612
  0.7 7.9 %copy-start.3 = (s32[1,128,128]{2,1,0:T(8,128)S(1)}, s32[1,128,128]{2,1,0:T(8,128)}, u32[]{:S(2)}) copy-start(s32[1,128,128]{2,1,0:T(8,128)} %param.20) | copy-start | bytes 196612
  0.7 7.9 %copy-start.2 = (s32[1,128,128]{2,1,0:T(8,128)S(1)}, s32[1,128,128]{2,1,0:T(8,128)}, u32[]{:S(2)}) copy-start(s32[1,128,128]{2,1,0:T(8,128)} %param.19) | copy-start | bytes 196612
  0.7 19.8 %copy-start = (s32[8,16,1024]{2,1,0:T(8,128)S(1)}, s32[8,16,1024]{2,1,0:T(8,128)}, u32[]{:S(2)}) copy-start(s32[8,16,1024]{2,1,0:T(8,128)} %solid.3) | copy-start | bytes 1572868
  3.2 12.9 %collective-permute-start.1 = (f32[5,8,1024]{2,1,0:T(8,128)}, f32[5,8,1024]{2,1,0:T(8,128)S(1)}, u32[]{:S(2)}, u32[]{:S(2)}) collective-permute-start(f32[5,8,1024]{2,1,0:T(8,128)} %get-tuple-element.77), channel_id=1, source_target_pairs={{0,1},{1,2},{2,3},{3,4},{4,5},{5,6},{6,7},{8,9},{9,10},{10,11},{11... | collective-permute-start | bytes 491528 | tf_op jit(solution)/shard_map/ppermute | solution.py:730
  7.2 9.1 %collective-permute-start = (f32[5,8,1024]{2,1,0:T(8,128)}, f32[5,8,1024]{2,1,0:T(8,128)S(1)}, u32[]{:S(2)}, u32[]{:S(2)}) collective-permute-start(f32[5,8,1024]{2,1,0:T(8,128)} %get-tuple-element.76), channel_id=1, source_target_pairs={{1,0},{2,1},{3,2},{4,3},{5,4},{6,5},{7,6},{9,8},{10,9},{11,10},{12... | collective-permute-start | bytes 491528 | tf_op jit(solution)/shard_map/ppermute | solution.py:729
  16.7 20.6 %collective-permute-start.2 = (f32[5,16,1024]{2,1,0:T(8,128)S(1)}, f32[5,16,1024]{2,1,0:T(8,128)S(1)}, u32[]{:S(2)}, u32[]{:S(2)}) collective-permute-start(f32[5,16,1024]{2,1,0:T(8,128)S(1)} %scatter.15), channel_id=1, source_target_pairs={{0,120},{8,0},{16,8},{24,16},{32,24},{40,32},{48,40},{56,48},{64,5... | collective-permute-start | bytes 983048 | tf_op jit(solution)/shard_map/ppermute | solution.py:737
  17.7 19.5 %collective-permute-start.3 = (f32[5,16,1024]{2,1,0:T(8,128)S(1)}, f32[5,16,1024]{2,1,0:T(8,128)S(1)}, u32[]{:S(2)}, u32[]{:S(2)}) collective-permute-start(f32[5,16,1024]{2,1,0:T(8,128)S(1)} %scatter.19), channel_id=1, source_target_pairs={{0,8},{8,16},{16,24},{24,32},{32,40},{40,48},{48,56},{56,64},{64,7... | collective-permute-start | bytes 983048 | tf_op jit(solution)/shard_map/ppermute | solution.py:738
  20.5 37.6 %copy-start.5 = (s32[1,128,128]{2,1,0:T(8,128)S(1)}, s32[1,128,128]{2,1,0:T(8,128)}, u32[]{:S(2)}) copy-start(s32[1,128,128]{2,1,0:T(8,128)} %param.23) | copy-start | bytes 196612
  37.3 20.8 %copy-start.1 = (f32[5,16,1024]{2,1,0:T(8,128)}, f32[5,16,1024]{2,1,0:T(8,128)S(1)}, u32[]{:S(2)}) copy-start(f32[5,16,1024]{2,1,0:T(8,128)S(1)} %collective-permute-done.3.h_dn) | copy-start | bytes 983044
  42.6 25.1 %all-to-all-start = ((f32[128,1,128]{2,1,0:T(1,128)}), f32[128,1,128]{2,1,0:T(1,128)S(1)}, u32[]{:S(2)}, u32[]{:S(2)}) async-start(f32[128,1,128]{2,1,0:T(1,128)} %bitcast.9), calls=%async_computation | async-start | bytes 131072 | tf_op jit(solution)/shard_map/all_to_all | solution.py:744

commit v4 on v3

--- a/solution.py
+++ b/solution.py
@@ -336,15 +336,18 @@
     return jnp.sum(acc, axis=0, keepdims=True)
 
 
-def pick_rest(start, listed, index, table, lidx, picked):
-    total = listed[2 * LISTED - 1]
-
+def pick_some(first, last, listed, index, table, lidx, picked):
     def turn(m, carry):
         for q in range(PER_TURN):
             pick(listed[m * PER_TURN + q], index, table, lidx, picked)
         return carry
 
-    lax.fori_loop(start // PER_TURN, (total + PER_TURN - 1) // PER_TURN, turn, 0)
+    lax.fori_loop(first, last, turn, 0)
+
+
+def pick_rest(start, listed, index, table, lidx, picked):
+    total = listed[2 * LISTED - 1]
+    pick_some(start // PER_TURN, (total + PER_TURN - 1) // PER_TURN, listed, index, table, lidx, picked)
 
 
 def fill_rims(v_up, v_dn, vup, vdn):
@@ -370,7 +373,8 @@
     )
 
 
-BESIDE = 27
+AHEAD = 3 * PER_TURN
+BESIDE = 25
 
 
 def scalar_copies(index_ref, listed_ref, index, listed, sem):
@@ -420,25 +424,12 @@
         for xt in range(COLS):
             collide_column(pull, xt, sav, sol, obuf, n)
             for q in range(BESIDE):
-                pick(listed[(n * COLS + xt) * BESIDE + q], index, table, lidx, picked)
+                pick(listed[AHEAD + (n * COLS + xt) * BESIDE + q], index, table, lidx, picked)
         pltpu.make_async_copy(obuf.at[:, n], out.at[:, n + 1], out_sem.at[n]).start()
         return carry
 
     for c in scalars:
         c.wait()
-    for q in range(IN_CHUNKS):
-        for c in copies[q]:
-            c.wait()
-        lax.fori_loop(IN_STEP * q, IN_STEP * (q + 1), slab, 0)
-    pick_rest(INNER * COLS * BESIDE, listed, index, table, lidx, picked)
-
-    def turn(b, carry):
-        for q in range(16):
-            t = b * 16 + q
-            local[pl.ds(t, 1), :] = placed(t, range(GROUPS), pos, picked)
-        return carry
-
-    lax.fori_loop(0, OWNERS // 16, turn, 0)
     for side, s in ((0, 0), (1, CS - 1)):
         for k, p in enumerate(SPAN_PAIRS):
             at = (side * 5 + k) * 128
@@ -449,6 +440,20 @@
                 at = 2 * SIDE_ROWS + ((side * 5 + k) * 8 + xt) * 8
                 own = p * 1024 + (71 if side == 1 else 0) + 8 * xt
                 near[at : at + 8, :] = table[pl.ds(own, CS, stride=128), :]
+    pick_some(0, AHEAD // PER_TURN, listed, index, table, lidx, picked)
+    for q in range(IN_CHUNKS):
+        for c in copies[q]:
+            c.wait()
+        lax.fori_loop(IN_STEP * q, IN_STEP * (q + 1), slab, 0)
+    pick_rest(AHEAD + INNER * COLS * BESIDE, listed, index, table, lidx, picked)
+
+    def turn(b, carry):
+        for q in range(16):
+            t = b * 16 + q
+            local[pl.ds(t, 1), :] = placed(t, range(GROUPS), pos, picked)
+        return carry
+
+    lax.fori_loop(0, OWNERS // 16, turn, 0)
     for n in range(INNER):
         pltpu.make_async_copy(obuf.at[:, n], out.at[:, n + 1], out_sem.at[n]).wait()
 

time: 69.8 us -> 69.3 us (level)
  starting transfers between devices: 24.5 us -> 22 us
  Pallas kernels: 39.3 us -> 40.6 us
    all_to_all x1, starting transfers between devices: 15.4 us -> 13 us  [body(): lax.all_to_all(values[:, None, :], ('span', 'vert'), split_axis=0, concat...]
    pallas_call x1, Pallas kernels: 5.3 us -> 6.57 us  [rim_call(): pl.pallas_call(rim_kernel, out_shape=shape(GRID), in_specs=[VMEM] * 11, o...]
  transfers between devices with their start and end apart: 5 -> 5, of which waited for: 1 -> 1; matrix products, arithmetic and copies ran while one was open for 0% -> 0% of each run, Pallas kernels for 42% -> 43%
where the time goes in v4:
time: 69.3 us; the launch traced here: 68.7 us
  Pallas kernels  40.6 us (59%)
  starting transfers between devices  22 us (32%)
  waiting for transfers between devices  4.69 us (7%)
  between operations  0.87 us (1%)
    pallas_call x1, Pallas kernels, inner_call(): pl.pallas_call(inner_kernel, out_shape=(shape((Q, CS, CV, NX)), shape(GRI...  16.9 us
    all_to_all x1, starting transfers between devices, body(): lax.all_to_all(values[:, None, :], ('span', 'vert'), split_axis=0, concat...  13 us
    pallas_call x1, Pallas kernels, tables_call(): pl.pallas_call(tables_kernel, out_shape=(shape((PAIRS, ROWS // PAIRS, LAN...  7.59 us
    pallas_call x1, Pallas kernels, rim_call(): pl.pallas_call(rim_kernel, out_shape=shape(GRID), in_specs=[VMEM] * 11, o...  6.57 us
    pallas_call x1, Pallas kernels, outer_call(): pl.pallas_call(outer_kernel, out_shape=(shape((Q, CS, CV, NX)), shape(GRI...  4.99 us
    all_to_all x1, waiting for transfers between devices, body(): lax.all_to_all(values[:, None, :], ('span', 'vert'), split_axis=0, concat...  4.68 us
    ppermute x1, starting transfers between devices, body(): v_dn = lax.ppermute(hv_dn, 'vert', [(i, i + 1) for i in range(nv - 1)])  3.95 us
    ppermute x1, starting transfers between devices, body(): h_dn = lax.ppermute(hs_dn, 'span', [(i, (i + 1) % ns) for i in range(ns)])  2.71 us
  transfers between devices with their start and end apart: 5, of which 1 were waited for; matrix products, arithmetic and copies ran while one was open for 0% of the time, Pallas kernels for 43%

profile of v4, /device:TPU:1, one launch (start us, length us, event | category | flops | bytes accessed | tf_op | source)
XLA Modules:
  0.0 68.7 jit_solution(15630758758712737043)
XLA Ops:
  0.6 0.0 copy-start.6
  0.6 0.0 copy-start.4
  0.7 0.0 copy-start.3
  0.7 0.0 copy-start.2
  0.7 0.0 copy-start
  0.7 2.5 %faces.1 = (f32[5,8,1024]{2,1,0:T(8,128)}, f32[5,8,1024]{2,1,0:T(8,128)}) custom-call(f32[19,8,16,1024]{3,2,1,0:T(8,128)} %adj.7), custom_call_target="tpu_custom_call" | custom-call | bytes 6000000 | tf_op jit(solution)/shard_map/faces/pallas_call | solution.py:612
  3.2 4.0 %collective-permute-start.1 = (f32[5,8,1024]{2,1,0:T(8,128)}, f32[5,8,1024]{2,1,0:T(8,128)S(1)}, u32[]{:S(2)}, u32[]{:S(2)}) collective-permute-start(f32[5,8,1024]{2,1,0:T(8,128)} %get-tuple-element.77), channel_id=1, source_target_pairs={{0,1},{1,2},{2,3},{3,4},{4,5},{5,6},{6,7},{8,9},{9,10},{10,11},{11... | collective-permute-start | bytes 491528 | tf_op jit(solution)/shard_map/ppermute | solution.py:735
  7.2 1.3 %collective-permute-start = (f32[5,8,1024]{2,1,0:T(8,128)}, f32[5,8,1024]{2,1,0:T(8,128)S(1)}, u32[]{:S(2)}, u32[]{:S(2)}) collective-permute-start(f32[5,8,1024]{2,1,0:T(8,128)} %get-tuple-element.76), channel_id=1, source_target_pairs={{1,0},{2,1},{3,2},{4,3},{5,4},{6,5},{7,6},{9,8},{10,9},{11,10},{12... | collective-permute-start | bytes 491528 | tf_op jit(solution)/shard_map/ppermute | solution.py:734
  8.5 0.0 copy-done.6
  8.5 0.0 copy-done.4
  8.5 0.0 copy-done.3
  8.5 0.0 copy-done.2
  8.5 7.6 %tables.1 = (f32[9,1024,128]{2,1,0:T(8,128)}, f32[5,16,1024]{2,1,0:T(8,128)S(1)}, f32[5,16,1024]{2,1,0:T(8,128)S(1)}, s32[128,128]{1,0:T(8,128)S(1)}, s32[128,12...) custom-call(s32[128,128]{1,0:T(8,128)S(1)} %bitcast.11, ...), custom_call_target="tpu_custom_call" | custom-call | bytes 24000000 | tf_op jit(solution)/shard_map/tables/pallas_call | solution.py:625
  16.1 0.0 collective-permute-done.1.v_dn
  16.2 0.1 scatter.16
  16.3 0.0 collective-permute-done.v_up
  16.3 0.1 scatter.14
  16.4 0.1 scatter.19
  16.5 0.1 scatter.15
  16.7 1.1 %collective-permute-start.2 = (f32[5,16,1024]{2,1,0:T(8,128)S(1)}, f32[5,16,1024]{2,1,0:T(8,128)S(1)}, u32[]{:S(2)}, u32[]{:S(2)}) collective-permute-start(f32[5,16,1024]{2,1,0:T(8,128)S(1)} %scatter.15), channel_id=1, source_target_pairs={{0,120},{8,0},{16,8},{24,16},{32,24},{40,32},{48,40},{56,48},{64,5... | collective-permute-start | bytes 983048 | tf_op jit(solution)/shard_map/ppermute | solution.py:742
  17.7 2.7 %collective-permute-start.3 = (f32[5,16,1024]{2,1,0:T(8,128)S(1)}, f32[5,16,1024]{2,1,0:T(8,128)S(1)}, u32[]{:S(2)}, u32[]{:S(2)}) collective-permute-start(f32[5,16,1024]{2,1,0:T(8,128)S(1)} %scatter.19), channel_id=1, source_target_pairs={{0,8},{8,16},{16,24},{24,32},{32,40},{40,48},{48,56},{56,64},{64,7... | collective-permute-start | bytes 983048 | tf_op jit(solution)/shard_map/ppermute | solution.py:743
  20.4 0.0 copy-done
  20.5 0.0 copy-start.5
  20.5 16.9 %inner.1 = (f32[19,8,16,1024]{3,2,1,0:T(8,128)}, f32[128,128]{1,0:T(8,128)S(1)}, s32[128,128]{1,0:T(8,128)S(1)}, s32[128,128]{1,0:T(8,128)S(1)}, s32[40,128]{1,0:T(8,128)S(1)}, /*index=5*/f32[1920,128]{1,0:T(8,128)S(1)}) custom-call(s32[16384]{0:T(1024)S(1)} %bitcast.15, s32[5120]{0:T(1024)S(1)} %bitcast.17, s32[128,128]{1,0:T(8,128)S(1)} %get-tuple-element.84.lidx, ...), custom_call_target="tpu_custom_call" | custom-call | bytes 45000000 | tf_op jit(solution)/shard_map/inner/pallas_call | solution.py:652
  37.3 0.0 collective-permute-done.2.h_up
  37.4 0.0 collective-permute-done.3.h_dn
  37.4 0.0 copy-start.1
  37.4 6.6 %rim.1 = f32[128,128]{1,0:T(8,128)} custom-call(s32[16384]{0:T(1024)S(1)} %bitcast.16, s32[5120]{0:T(1024)S(1)} %bitcast.18, s32[128,128]{1,0:T(8,128)S(1)} %get-tuple-element.84.lidx, s32[128,128]{1,0:T(8,128)S(1)} %get-tuple-element.90.pos, f32[128,128]{1,0:T(8,128)S(1)} %get-tuple-element.91.weight, f32[128,128]{1,0:T(8,128)S(1)} %get-tuple-element.92.local, ...), custom_call_target="tpu_custom_call" | custom-call | bytes 15000000 | tf_op jit(solution)/shard_map/rim/pallas_call | solution.py:681
  44.0 13.0 %all-to-all-start = ((f32[128,1,128]{2,1,0:T(1,128)}), f32[128,1,128]{2,1,0:T(1,128)S(1)}, u32[]{:S(2)}, u32[]{:S(2)}) async-start(f32[128,1,128]{2,1,0:T(1,128)} %bitcast.9), calls=%async_computation | async-start | bytes 131072 | tf_op jit(solution)/shard_map/all_to_all | solution.py:749
  57.0 0.0 copy-done.1
  57.0 0.0 copy-done.5
  57.0 5.0 %outer.1 = (f32[19,8,16,1024]{3,2,1,0:T(8,128)}, s32[128,128]{1,0:T(8,128)S(1)}) custom-call(f32[5,16,1024]{2,1,0:T(8,128)S(1)} %collective-permute-done.2.h_up, f32[5,16,1024]{2,1,0:T(8,128)} %copy-done.1, f32[5,8,1024]{2,1,0:T(8,128)S(1)} %collective-permute-done.v_up, ...), custom_call_target="tpu_custom_call", output_to_operand_aliasing={{0}: (8, {})} | custom-call | bytes 9000000 | tf_op jit(solution)/shard_map/outer/pallas_call | solution.py:697
  62.0 4.7 %all-to-all-done.received = f32[128,1,128]{2,1,0:T(1,128)S(1)} async-done(((f32[128,1,128]{2,1,0:T(1,128)}), f32[128,1,128]{2,1,0:T(1,128)S(1)}, u32[]{:S(2)}, u32[]{:S(2)}) %all-to-all-start) | async-done | bytes 65568 | tf_op jit(solution)/shard_map/all_to_all | solution.py:749
  66.7 2.1 %element_sums.1 = f32[32,128]{1,0:T(8,128)} custom-call(s32[128,128]{1,0:T(8,128)S(1)} %get-tuple-element.98.slots, f32[128,1,128]{2,1,0:T(1,128)S(1)} %all-to-all-done.received), custom_call_target="tpu_custom_call" | custom-call | bytes 12000000 | tf_op jit(solution)/shard_map/element_sums/pallas_call | solution.py:719
  (2 shorter events, 0.0 us)
Async XLA Ops:
  0.6 7.9 %copy-start.6 = (s32[1,128]{1,0:T(1,128)S(1)}, s32[1,128]{1,0:T(1,128)}, u32[]{:S(2)}) copy-start(s32[1,128]{1,0:T(1,128)} %counts_ref.1) | copy-start | bytes 1540
  0.6 7.9 %copy-start.4 = (f32[1,128,128]{2,1,0:T(8,128)S(1)}, f32[1,128,128]{2,1,0:T(8,128)}, u32[]{:S(2)}) copy-start(f32[1,128,128]{2,1,0:T(8,128)} %param.21) | copy-start | bytes 196612
  0.7 7.9 %copy-start.3 = (s32[1,128,128]{2,1,0:T(8,128)S(1)}, s32[1,128,128]{2,1,0:T(8,128)}, u32[]{:S(2)}) copy-start(s32[1,128,128]{2,1,0:T(8,128)} %param.20) | copy-start | bytes 196612
  0.7 7.9 %copy-start.2 = (s32[1,128,128]{2,1,0:T(8,128)S(1)}, s32[1,128,128]{2,1,0:T(8,128)}, u32[]{:S(2)}) copy-start(s32[1,128,128]{2,1,0:T(8,128)} %param.19) | copy-start | bytes 196612
  0.7 19.8 %copy-start = (s32[8,16,1024]{2,1,0:T(8,128)S(1)}, s32[8,16,1024]{2,1,0:T(8,128)}, u32[]{:S(2)}) copy-start(s32[8,16,1024]{2,1,0:T(8,128)} %solid.3) | copy-start | bytes 1572868
  3.2 12.9 %collective-permute-start.1 = (f32[5,8,1024]{2,1,0:T(8,128)}, f32[5,8,1024]{2,1,0:T(8,128)S(1)}, u32[]{:S(2)}, u32[]{:S(2)}) collective-permute-start(f32[5,8,1024]{2,1,0:T(8,128)} %get-tuple-element.77), channel_id=1, source_target_pairs={{0,1},{1,2},{2,3},{3,4},{4,5},{5,6},{6,7},{8,9},{9,10},{10,11},{11... | collective-permute-start | bytes 491528 | tf_op jit(solution)/shard_map/ppermute | solution.py:735
  7.2 9.1 %collective-permute-start = (f32[5,8,1024]{2,1,0:T(8,128)}, f32[5,8,1024]{2,1,0:T(8,128)S(1)}, u32[]{:S(2)}, u32[]{:S(2)}) collective-permute-start(f32[5,8,1024]{2,1,0:T(8,128)} %get-tuple-element.76), channel_id=1, source_target_pairs={{1,0},{2,1},{3,2},{4,3},{5,4},{6,5},{7,6},{9,8},{10,9},{11,10},{12... | collective-permute-start | bytes 491528 | tf_op jit(solution)/shard_map/ppermute | solution.py:734
  16.7 20.7 %collective-permute-start.2 = (f32[5,16,1024]{2,1,0:T(8,128)S(1)}, f32[5,16,1024]{2,1,0:T(8,128)S(1)}, u32[]{:S(2)}, u32[]{:S(2)}) collective-permute-start(f32[5,16,1024]{2,1,0:T(8,128)S(1)} %scatter.15), channel_id=1, source_target_pairs={{0,120},{8,0},{16,8},{24,16},{32,24},{40,32},{48,40},{56,48},{64,5... | collective-permute-start | bytes 983048 | tf_op jit(solution)/shard_map/ppermute | solution.py:742
  17.7 19.6 %collective-permute-start.3 = (f32[5,16,1024]{2,1,0:T(8,128)S(1)}, f32[5,16,1024]{2,1,0:T(8,128)S(1)}, u32[]{:S(2)}, u32[]{:S(2)}) collective-permute-start(f32[5,16,1024]{2,1,0:T(8,128)S(1)} %scatter.19), channel_id=1, source_target_pairs={{0,8},{8,16},{16,24},{24,32},{32,40},{40,48},{48,56},{56,64},{64,7... | collective-permute-start | bytes 983048 | tf_op jit(solution)/shard_map/ppermute | solution.py:743
  20.5 36.5 %copy-start.5 = (s32[1,128,128]{2,1,0:T(8,128)S(1)}, s32[1,128,128]{2,1,0:T(8,128)}, u32[]{:S(2)}) copy-start(s32[1,128,128]{2,1,0:T(8,128)} %param.23) | copy-start | bytes 196612
  37.4 19.6 %copy-start.1 = (f32[5,16,1024]{2,1,0:T(8,128)}, f32[5,16,1024]{2,1,0:T(8,128)S(1)}, u32[]{:S(2)}) copy-start(f32[5,16,1024]{2,1,0:T(8,128)S(1)} %collective-permute-done.3.h_dn) | copy-start | bytes 983044
  44.0 22.7 %all-to-all-start = ((f32[128,1,128]{2,1,0:T(1,128)}), f32[128,1,128]{2,1,0:T(1,128)S(1)}, u32[]{:S(2)}, u32[]{:S(2)}) async-start(f32[128,1,128]{2,1,0:T(1,128)} %bitcast.9), calls=%async_computation | async-start | bytes 131072 | tf_op jit(solution)/shard_map/all_to_all | solution.py:749

commit v5 on v4

--- a/solution.py
+++ b/solution.py
@@ -357,13 +357,15 @@
                 rims[k, xt] = halo[k, :, col(xt)]
 
 
-def collide_column(pull, xt, sav, sol, obuf, s):
+def collide_column(pull, xt, sav, sol, obuf, s, beside=None):
     pulled = [pull(i, xt) for i in range(Q)]
     sums = [pulled[2 * p + 1] + pulled[2 * p + 2] for p in range(PAIRS)]
     diffs = [pulled[2 * p + 1] - pulled[2 * p + 2] for p in range(PAIRS)]
 
     def store(i, v):
         obuf[i, s, :, col(xt)] = v
+        if beside is not None:
+            beside(i)
 
     collide(
         pulled, sums, diffs,
@@ -422,9 +424,14 @@
 
         pull = puller(column)
         for xt in range(COLS):
-            collide_column(pull, xt, sav, sol, obuf, n)
-            for q in range(BESIDE):
-                pick(listed[AHEAD + (n * COLS + xt) * BESIDE + q], index, table, lidx, picked)
+            first = AHEAD + (n * COLS + xt) * BESIDE
+
+            def beside(q):
+                pick(listed[first + q], index, table, lidx, picked)
+
+            for q in range(Q, BESIDE):
+                beside(q)
+            collide_column(pull, xt, sav, sol, obuf, n, beside)
         pltpu.make_async_copy(obuf.at[:, n], out.at[:, n + 1], out_sem.at[n]).start()
         return carry
 

time: 69.3 us -> 69.9 us (level)
  Pallas kernels: 40.6 us -> 41.5 us
where the time goes in v5:
time: 69.9 us; the launch traced here: 69.6 us
  Pallas kernels  41.5 us (59%)
  starting transfers between devices  22.1 us (32%)
  waiting for transfers between devices  4.69 us (7%)
  between operations  0.87 us (1%)
    pallas_call x1, Pallas kernels, inner_call(): pl.pallas_call(inner_kernel, out_shape=(shape((Q, CS, CV, NX)), shape(GRI...  17.5 us
    all_to_all x1, starting transfers between devices, body(): lax.all_to_all(values[:, None, :], ('span', 'vert'), split_axis=0, concat...  13 us
    pallas_call x1, Pallas kernels, tables_call(): pl.pallas_call(tables_kernel, out_shape=(shape((PAIRS, ROWS // PAIRS, LAN...  7.59 us
    pallas_call x1, Pallas kernels, rim_call(): pl.pallas_call(rim_kernel, out_shape=shape(GRID), in_specs=[VMEM] * 11, o...  6.88 us
    pallas_call x1, Pallas kernels, outer_call(): pl.pallas_call(outer_kernel, out_shape=(shape((Q, CS, CV, NX)), shape(GRI...  4.99 us
    all_to_all x1, waiting for transfers between devices, body(): lax.all_to_all(values[:, None, :], ('span', 'vert'), split_axis=0, concat...  4.68 us
    ppermute x1, starting transfers between devices, body(): v_dn = lax.ppermute(hv_dn, 'vert', [(i, i + 1) for i in range(nv - 1)])  3.95 us
    ppermute x1, starting transfers between devices, body(): h_dn = lax.ppermute(hs_dn, 'span', [(i, (i + 1) % ns) for i in range(ns)])  2.71 us
  transfers between devices with their start and end apart: 5, of which 1 were waited for; matrix products, arithmetic and copies ran while one was open for 0% of the time, Pallas kernels for 43%

profile of v5, /device:TPU:1, one launch (start us, length us, event | category | flops | bytes accessed | tf_op | source)
XLA Modules:
  0.0 69.6 jit_solution(14514962430004417962)
XLA Ops:
  0.6 0.0 copy-start.6
  0.6 0.0 copy-start.4
  0.7 0.0 copy-start.3
  0.7 0.0 copy-start.2
  0.7 0.0 copy-start
  0.7 2.5 %faces.1 = (f32[5,8,1024]{2,1,0:T(8,128)}, f32[5,8,1024]{2,1,0:T(8,128)}) custom-call(f32[19,8,16,1024]{3,2,1,0:T(8,128)} %adj.7), custom_call_target="tpu_custom_call" | custom-call | bytes 6000000 | tf_op jit(solution)/shard_map/faces/pallas_call | solution.py:619
  3.2 4.0 %collective-permute-start.1 = (f32[5,8,1024]{2,1,0:T(8,128)}, f32[5,8,1024]{2,1,0:T(8,128)S(1)}, u32[]{:S(2)}, u32[]{:S(2)}) collective-permute-start(f32[5,8,1024]{2,1,0:T(8,128)} %get-tuple-element.77), channel_id=1, source_target_pairs={{0,1},{1,2},{2,3},{3,4},{4,5},{5,6},{6,7},{8,9},{9,10},{10,11},{11... | collective-permute-start | bytes 491528 | tf_op jit(solution)/shard_map/ppermute | solution.py:742
  7.2 1.3 %collective-permute-start = (f32[5,8,1024]{2,1,0:T(8,128)}, f32[5,8,1024]{2,1,0:T(8,128)S(1)}, u32[]{:S(2)}, u32[]{:S(2)}) collective-permute-start(f32[5,8,1024]{2,1,0:T(8,128)} %get-tuple-element.76), channel_id=1, source_target_pairs={{1,0},{2,1},{3,2},{4,3},{5,4},{6,5},{7,6},{9,8},{10,9},{11,10},{12... | collective-permute-start | bytes 491528 | tf_op jit(solution)/shard_map/ppermute | solution.py:741
  8.5 0.0 copy-done.6
  8.5 0.0 copy-done.4
  8.5 0.0 copy-done.3
  8.5 0.0 copy-done.2
  8.5 7.6 %tables.1 = (f32[9,1024,128]{2,1,0:T(8,128)}, f32[5,16,1024]{2,1,0:T(8,128)S(1)}, f32[5,16,1024]{2,1,0:T(8,128)S(1)}, s32[128,128]{1,0:T(8,128)S(1)}, s32[128,12...) custom-call(s32[128,128]{1,0:T(8,128)S(1)} %bitcast.11, ...), custom_call_target="tpu_custom_call" | custom-call | bytes 24000000 | tf_op jit(solution)/shard_map/tables/pallas_call | solution.py:632
  16.1 0.0 collective-permute-done.1.v_dn
  16.2 0.1 scatter.16
  16.3 0.0 collective-permute-done.v_up
  16.3 0.1 scatter.14
  16.4 0.1 scatter.19
  16.5 0.1 scatter.15
  16.7 1.1 %collective-permute-start.2 = (f32[5,16,1024]{2,1,0:T(8,128)S(1)}, f32[5,16,1024]{2,1,0:T(8,128)S(1)}, u32[]{:S(2)}, u32[]{:S(2)}) collective-permute-start(f32[5,16,1024]{2,1,0:T(8,128)S(1)} %scatter.15), channel_id=1, source_target_pairs={{0,120},{8,0},{16,8},{24,16},{32,24},{40,32},{48,40},{56,48},{64,5... | collective-permute-start | bytes 983048 | tf_op jit(solution)/shard_map/ppermute | solution.py:749
  17.7 2.7 %collective-permute-start.3 = (f32[5,16,1024]{2,1,0:T(8,128)S(1)}, f32[5,16,1024]{2,1,0:T(8,128)S(1)}, u32[]{:S(2)}, u32[]{:S(2)}) collective-permute-start(f32[5,16,1024]{2,1,0:T(8,128)S(1)} %scatter.19), channel_id=1, source_target_pairs={{0,8},{8,16},{16,24},{24,32},{32,40},{40,48},{48,56},{56,64},{64,7... | collective-permute-start | bytes 983048 | tf_op jit(solution)/shard_map/ppermute | solution.py:750
  20.4 0.0 copy-done
  20.5 0.0 copy-start.5
  20.5 17.5 %inner.1 = (f32[19,8,16,1024]{3,2,1,0:T(8,128)}, f32[128,128]{1,0:T(8,128)S(1)}, s32[128,128]{1,0:T(8,128)S(1)}, s32[128,128]{1,0:T(8,128)S(1)}, s32[40,128]{1,0:T(8,128)S(1)}, /*index=5*/f32[1920,128]{1,0:T(8,128)S(1)}) custom-call(s32[16384]{0:T(1024)S(1)} %bitcast.15, s32[5120]{0:T(1024)S(1)} %bitcast.17, s32[128,128]{1,0:T(8,128)S(1)} %get-tuple-element.84.lidx, ...), custom_call_target="tpu_custom_call" | custom-call | bytes 45000000 | tf_op jit(solution)/shard_map/inner/pallas_call | solution.py:659
  37.9 0.0 collective-permute-done.2.h_up
  37.9 0.0 collective-permute-done.3.h_dn
  37.9 0.0 copy-start.1
  38.0 6.9 %rim.1 = f32[128,128]{1,0:T(8,128)} custom-call(s32[16384]{0:T(1024)S(1)} %bitcast.16, s32[5120]{0:T(1024)S(1)} %bitcast.18, s32[128,128]{1,0:T(8,128)S(1)} %get-tuple-element.84.lidx, s32[128,128]{1,0:T(8,128)S(1)} %get-tuple-element.90.pos, f32[128,128]{1,0:T(8,128)S(1)} %get-tuple-element.91.weight, f32[128,128]{1,0:T(8,128)S(1)} %get-tuple-element.92.local, ...), custom_call_target="tpu_custom_call" | custom-call | bytes 15000000 | tf_op jit(solution)/shard_map/rim/pallas_call | solution.py:688
  44.8 13.0 %all-to-all-start = ((f32[128,1,128]{2,1,0:T(1,128)}), f32[128,1,128]{2,1,0:T(1,128)S(1)}, u32[]{:S(2)}, u32[]{:S(2)}) async-start(f32[128,1,128]{2,1,0:T(1,128)} %bitcast.9), calls=%async_computation | async-start | bytes 131072 | tf_op jit(solution)/shard_map/all_to_all | solution.py:756
  57.9 0.0 copy-done.1
  57.9 0.0 copy-done.5
  57.9 5.0 %outer.1 = (f32[19,8,16,1024]{3,2,1,0:T(8,128)}, s32[128,128]{1,0:T(8,128)S(1)}) custom-call(f32[5,16,1024]{2,1,0:T(8,128)S(1)} %collective-permute-done.2.h_up, f32[5,16,1024]{2,1,0:T(8,128)} %copy-done.1, f32[5,8,1024]{2,1,0:T(8,128)S(1)} %collective-permute-done.v_up, ...), custom_call_target="tpu_custom_call", output_to_operand_aliasing={{0}: (8, {})} | custom-call | bytes 9000000 | tf_op jit(solution)/shard_map/outer/pallas_call | solution.py:704
  62.9 4.7 %all-to-all-done.received = f32[128,1,128]{2,1,0:T(1,128)S(1)} async-done(((f32[128,1,128]{2,1,0:T(1,128)}), f32[128,1,128]{2,1,0:T(1,128)S(1)}, u32[]{:S(2)}, u32[]{:S(2)}) %all-to-all-start) | async-done | bytes 65568 | tf_op jit(solution)/shard_map/all_to_all | solution.py:756
  67.6 2.1 %element_sums.1 = f32[32,128]{1,0:T(8,128)} custom-call(s32[128,128]{1,0:T(8,128)S(1)} %get-tuple-element.98.slots, f32[128,1,128]{2,1,0:T(1,128)S(1)} %all-to-all-done.received), custom_call_target="tpu_custom_call" | custom-call | bytes 12000000 | tf_op jit(solution)/shard_map/element_sums/pallas_call | solution.py:726
  (2 shorter events, 0.0 us)
Async XLA Ops:
  0.6 7.9 %copy-start.6 = (s32[1,128]{1,0:T(1,128)S(1)}, s32[1,128]{1,0:T(1,128)}, u32[]{:S(2)}) copy-start(s32[1,128]{1,0:T(1,128)} %counts_ref.1) | copy-start | bytes 1540
  0.6 7.9 %copy-start.4 = (f32[1,128,128]{2,1,0:T(8,128)S(1)}, f32[1,128,128]{2,1,0:T(8,128)}, u32[]{:S(2)}) copy-start(f32[1,128,128]{2,1,0:T(8,128)} %param.21) | copy-start | bytes 196612
  0.7 7.9 %copy-start.3 = (s32[1,128,128]{2,1,0:T(8,128)S(1)}, s32[1,128,128]{2,1,0:T(8,128)}, u32[]{:S(2)}) copy-start(s32[1,128,128]{2,1,0:T(8,128)} %param.20) | copy-start | bytes 196612
  0.7 7.9 %copy-start.2 = (s32[1,128,128]{2,1,0:T(8,128)S(1)}, s32[1,128,128]{2,1,0:T(8,128)}, u32[]{:S(2)}) copy-start(s32[1,128,128]{2,1,0:T(8,128)} %param.19) | copy-start | bytes 196612
  0.7 19.8 %copy-start = (s32[8,16,1024]{2,1,0:T(8,128)S(1)}, s32[8,16,1024]{2,1,0:T(8,128)}, u32[]{:S(2)}) copy-start(s32[8,16,1024]{2,1,0:T(8,128)} %solid.3) | copy-start | bytes 1572868
  3.2 12.9 %collective-permute-start.1 = (f32[5,8,1024]{2,1,0:T(8,128)}, f32[5,8,1024]{2,1,0:T(8,128)S(1)}, u32[]{:S(2)}, u32[]{:S(2)}) collective-permute-start(f32[5,8,1024]{2,1,0:T(8,128)} %get-tuple-element.77), channel_id=1, source_target_pairs={{0,1},{1,2},{2,3},{3,4},{4,5},{5,6},{6,7},{8,9},{9,10},{10,11},{11... | collective-permute-start | bytes 491528 | tf_op jit(solution)/shard_map/ppermute | solution.py:742
  7.2 9.1 %collective-permute-start = (f32[5,8,1024]{2,1,0:T(8,128)}, f32[5,8,1024]{2,1,0:T(8,128)S(1)}, u32[]{:S(2)}, u32[]{:S(2)}) collective-permute-start(f32[5,8,1024]{2,1,0:T(8,128)} %get-tuple-element.76), channel_id=1, source_target_pairs={{1,0},{2,1},{3,2},{4,3},{5,4},{6,5},{7,6},{9,8},{10,9},{11,10},{12... | collective-permute-start | bytes 491528 | tf_op jit(solution)/shard_map/ppermute | solution.py:741
  16.7 21.3 %collective-permute-start.2 = (f32[5,16,1024]{2,1,0:T(8,128)S(1)}, f32[5,16,1024]{2,1,0:T(8,128)S(1)}, u32[]{:S(2)}, u32[]{:S(2)}) collective-permute-start(f32[5,16,1024]{2,1,0:T(8,128)S(1)} %scatter.15), channel_id=1, source_target_pairs={{0,120},{8,0},{16,8},{24,16},{32,24},{40,32},{48,40},{56,48},{64,5... | collective-permute-start | bytes 983048 | tf_op jit(solution)/shard_map/ppermute | solution.py:749
  17.7 20.2 %collective-permute-start.3 = (f32[5,16,1024]{2,1,0:T(8,128)S(1)}, f32[5,16,1024]{2,1,0:T(8,128)S(1)}, u32[]{:S(2)}, u32[]{:S(2)}) collective-permute-start(f32[5,16,1024]{2,1,0:T(8,128)S(1)} %scatter.19), channel_id=1, source_target_pairs={{0,8},{8,16},{16,24},{24,32},{32,40},{40,48},{48,56},{56,64},{64,7... | collective-permute-start | bytes 983048 | tf_op jit(solution)/shard_map/ppermute | solution.py:750
  20.5 37.4 %copy-start.5 = (s32[1,128,128]{2,1,0:T(8,128)S(1)}, s32[1,128,128]{2,1,0:T(8,128)}, u32[]{:S(2)}) copy-start(s32[1,128,128]{2,1,0:T(8,128)} %param.23) | copy-start | bytes 196612
  37.9 19.9 %copy-start.1 = (f32[5,16,1024]{2,1,0:T(8,128)}, f32[5,16,1024]{2,1,0:T(8,128)S(1)}, u32[]{:S(2)}) copy-start(f32[5,16,1024]{2,1,0:T(8,128)S(1)} %collective-permute-done.3.h_dn) | copy-start | bytes 983044
  44.8 22.7 %all-to-all-start = ((f32[128,1,128]{2,1,0:T(1,128)}), f32[128,1,128]{2,1,0:T(1,128)S(1)}, u32[]{:S(2)}, u32[]{:S(2)}) async-start(f32[128,1,128]{2,1,0:T(1,128)} %bitcast.9), calls=%async_computation | async-start | bytes 131072 | tf_op jit(solution)/shard_map/all_to_all | solution.py:756
